TPU v7x, 256 devices: a whole 4x4x8 slice. The times are simulated.
256 devices in a mesh: row: 8 (over z_lo, core), col: 32 (over x, z_hi, y).
Axes of the slice: x: 4, y: 4, z: 8 (z_hi: 2, z_lo: 4; z = z_hi * 4 + z_lo), core: 2. Of those that a mesh axis runs over, the one named last changes fastest.
Arguments:
- features: bfloat16 [65536, 128], P(('row', 'col')), may hold values from -6 to 6
- weight: bfloat16 [128, 256], replicated, may hold values from -0.5 to 0.5
- bias_vector: float32 [256], replicated, may hold values from -3 to 3
- cotangent: bfloat16 [65536, 256], P(('row', 'col')), may hold values from -6 to 6
- degrees: int32 [65536], P(('row', 'col')), may hold values from 1 to 255
- adjacency_tiles: bfloat16 [8, 32, 128, 128, 128], P('row', 'col'), may hold values from 0 to 1, as said below
- tile_positions: int32 [8, 32, 128], P('row', 'col'), may hold values from 0 to 1023, as said below
- tile_counts: int32 [8, 32], P('row', 'col'), may hold values from 16 to 128, as said below
Outputs:
- activations: bfloat16 [65536, 256], P(('row', 'col'))
- grad_features: bfloat16 [65536, 128], P(('row', 'col'))
- grad_weight: float32 [128, 256], replicated
- grad_bias: float32 [256], replicated
Inputs may be any that keep to these rules, and one draw needn't show every extreme that they name: `tile_positions`: the first tile_counts[r, c] positions of device (r, c) are distinct; each position q stands for row block q // 16 and column block q % 16 of that device. `tile_counts`: some device has all 128 slots live. `adjacency_tiles`: entries are 0 or 1.
All inputs are finite; a program needn't handle non-finite values.
Results may differ from a plain program's by a relative error of at most 0.015.
Values may be sent and summed in bfloat16 or wider, within the bound.
A program may use at most 128 MiB of HBM per device.

v0:
```python
import jax
import jax.numpy as jnp
from jax import lax
from jax.sharding import PartitionSpec as P

BLOCK = 128


def split_three(values):
    upper = values.astype(jnp.bfloat16)
    rest = values - upper.astype(jnp.float32)
    middle = rest.astype(jnp.bfloat16)
    lower = (rest - middle.astype(jnp.float32)).astype(jnp.bfloat16)
    return (upper, middle, lower)


def spread(contrib, targets, active, slots, columns):
    selector = (
        (targets[None, :] == jnp.arange(slots, dtype=jnp.int32)[:, None]).astype(jnp.float32)
        * active[None, :]
    ).astype(jnp.bfloat16)
    flattened = contrib.reshape(contrib.shape[0], -1)
    pieces = split_three(flattened)
    summed = jnp.dot(selector, pieces[0], preferred_element_type=jnp.float32)
    summed = summed + jnp.dot(selector, pieces[1], preferred_element_type=jnp.float32)
    summed = summed + jnp.dot(selector, pieces[2], preferred_element_type=jnp.float32)
    return summed.reshape(slots * BLOCK, columns)


def tile_product(form, tile_data, picked):
    if picked.dtype == jnp.bfloat16:
        return jnp.einsum(form, tile_data, picked, preferred_element_type=jnp.float32)
    pieces = split_three(picked)
    first = jnp.einsum(form, tile_data, pieces[0], preferred_element_type=jnp.float32)
    second = jnp.einsum(form, tile_data, pieces[1], preferred_element_type=jnp.float32)
    third = jnp.einsum(form, tile_data, pieces[2], preferred_element_type=jnp.float32)
    return first + second + third


def per_device(
    features, weight, bias_vector, cotangent, degrees, adjacency_tiles, tile_positions, tile_counts
):
    tile_data = adjacency_tiles[0, 0]
    positions = tile_positions[0, 0]
    tile_total = tile_counts[0, 0]
    row_devices = lax.axis_size("row")
    col_devices = lax.axis_size("col")
    local_rows = features.shape[0]
    per_part = local_rows // BLOCK
    col_slots = row_devices * per_part
    row_slots = col_devices * per_part
    row_block = positions // col_slots
    col_block = positions % col_slots
    capacity = tile_data.shape[0]
    active = (jnp.arange(capacity, dtype=jnp.int32) < tile_total).astype(jnp.float32)
    scale_rows = lax.rsqrt(degrees.astype(jnp.float32))[:, None]
    scaled = (scale_rows * features.astype(jnp.float32)).astype(jnp.bfloat16)
    weight_full = weight.astype(jnp.float32)
    gathered = lax.all_gather(scaled, "row", axis=0, tiled=True)
    picked = jnp.take(gathered.reshape(col_slots, BLOCK, scaled.shape[1]), col_block, axis=0)
    contrib = tile_product("tij,tjf->tif", tile_data, picked)
    partial_value = spread(contrib, row_block, active, row_slots, scaled.shape[1])
    summed = lax.psum_scatter(partial_value, "col", scatter_dimension=0, tiled=True)
    hidden = scale_rows * summed
    preact = jnp.dot(hidden, weight_full, precision=lax.Precision.HIGHEST) + bias_vector[None, :]
    logistic = jax.nn.sigmoid(preact)
    activations = (preact * logistic).astype(jnp.bfloat16)
    grad_pre = cotangent.astype(jnp.float32) * logistic * (1.0 + preact * (1.0 - logistic))
    outgoing = scale_rows * jnp.dot(grad_pre, weight_full.T, precision=lax.Precision.HIGHEST)
    columns = outgoing.shape[1]
    gathered_back = lax.all_gather(outgoing, "col", axis=0, tiled=True)
    picked_back = jnp.take(gathered_back.reshape(row_slots, BLOCK, columns), row_block, axis=0)
    contrib_back = tile_product("tji,tjf->tif", tile_data, picked_back)
    partial_back = spread(contrib_back, col_block, active, col_slots, columns)
    returned = lax.psum_scatter(partial_back, "row", scatter_dimension=0, tiled=True)
    weight_term = jnp.dot(hidden.T, grad_pre, precision=lax.Precision.HIGHEST)
    grad_weight, grad_bias = lax.psum((weight_term, jnp.sum(grad_pre, axis=0)), ("row", "col"))
    grad_features = (scale_rows * returned).astype(jnp.bfloat16)
    return (activations, grad_features, grad_weight, grad_bias)


def solution(mesh):
    placed = (
        P(("row", "col"), None),
        P(),
        P(),
        P(("row", "col"), None),
        P(("row", "col")),
        P("row", "col", None, None, None),
        P("row", "col", None),
        P("row", "col"),
    )
    return jax.shard_map(
        per_device,
        mesh=mesh,
        in_specs=placed,
        out_specs=(P(("row", "col"), None), P(("row", "col"), None), P(), P()),
        check_vma=False,
    )
```

profile of v0, /device:TPU:1, one launch (start us, length us, event | category | flops | bytes accessed | tf_op | source)
XLA Modules:
  0.0 792.5 jit_solution(4003984003503621814)
XLA Ops:
  7.2 0.0 copy-start
  7.2 0.0 reduce-scatter.3.cloned.1.call-start
  7.9 0.7 convert_rsqrt_fusion
  8.6 0.7 fusion.54
  9.2 0.7 compare_and_fusion
  9.9 0.9 multiply_convert_fusion.2
  10.9 17.8 %all_gather.6 = bf16[2048,128]{1,0:T(8,128)(2,1)S(1)} all-gather(bf16[256,128]{1,0:T(8,128)(2,1)S(1)} %multiply_convert_fusion.2), channel_id=1, replica_groups=mesh['row'=8,'col'=32] {'row'}, dimensions={0}, use_global_device_ids=true | all-gather | bytes 589824 | tf_op jit(solution)/shard_map/all_gather | solution.py:59
  28.6 3.0 gather_fusion
  31.7 9.9 %fusion.20 = f32[128,128,128]{1,2,0:T(8,128)} fusion(bf16[1,1,128,128,128]{4,3,2,1,0:T(8,128)(2,1)} %param.13, bf16[128,128,128]{2,1,0:T(8,128)(2,1)} %gather_fusion, pred[128]{0:T(512)(128)(4,1)S(1)} %get-tuple-element.17), kind=kOutput, calls=%fused_computation.35 | convolution fusion | flops 538968064 | bytes 16777344 | tf_op jit(solution)/shard_map/tij,tjf->tif/dot_general | solution.py:32
  41.6 9.3 %copy.13 = f32[128,128,128]{0,2,1:T(8,128)} copy(f32[128,128,128]{1,2,0:T(8,128)} %fusion.20) | data formatting | bytes 16777216 | tf_op jit(solution)/shard_map/tij,tjf->tif/dot_general | solution.py:32
  50.9 0.0 copy-start.3
  50.9 3.8 bitcast_convert_fusion.1
  54.7 2.0 copy-done.3
  56.7 1.9 subtract_convert_fusion.2
  58.6 1.6 fusion.33
  60.2 1.6 convolution_add_fusion.1
  61.8 3.5 convolution_add_fusion
  65.3 4.9 reshape.216
  70.2 0.0 copy-start.7
  70.2 0.0 copy-start.8
  70.2 0.0 reduce-scatter.3.cloned.1.call-update
  70.2 0.0 all-gather.2.cloned.1.call-start
  70.3 213.2 %reduce-scatter.3.cloned.1.call-done = f32[256,128]{1,0:T(8,128)} async-done(((f32[8192,128]{1,0:T(8,128)}), f32[256,128]{1,0:T(8,128)}) %reduce-scatter.3.cloned.1.call-update) | async-done | bytes 131088 | tf_op jit(solution)/shard_map/reduce_scatter | solution.py:63
  283.5 0.0 copy-done
  283.5 0.0 copy-done.7
  283.5 0.0 copy-done.8
  283.5 2.0 fusion.65
  285.4 0.9 convolution_multiply_fusion
  286.4 0.0 all-gather.2.cloned.1.call-update
  286.4 0.2 reduce-scatter.5.cloned.1.call-start
  286.6 124.9 %all-gather.2.cloned.1.call-done = f32[8192,128]{1,0:T(8,128)} async-done(((f32[256,128]{1,0:T(8,128)}), f32[8192,128]{1,0:T(8,128)}) %all-gather.2.cloned.1.call-update) | async-done | bytes 4194320 | tf_op jit(solution)/shard_map/all_gather | solution.py:71
  411.5 6.5 gather_fusion.1
  418.0 0.0 copy-start.2
  418.0 0.0 copy-start.5
  418.0 10.4 %fusion.4 = f32[128,128,128]{2,1,0:T(8,128)} fusion(f32[128,128,128]{2,1,0:T(8,128)} %gather_fusion.1, bf16[1,1,128,128,128]{4,3,2,1,0:T(8,128)(2,1)} %param.13, pred[128]{0:T(512)(128)(4,1)S(1)} %get-tuple-element.6), kind=kOutput, calls=%fused_computation.20 | convolution fusion | flops 547356672 | bytes 20971648 | tf_op jit(solution)/shard_map/tji,tjf->tif/dot_general | solution.py:35
  428.5 0.0 copy-done.2
  428.5 0.0 copy-done.5
  428.5 5.7 fusion
  434.2 15.1 %add_bitcast_fusion = f32[128,128,128]{1,2,0:T(8,128)} fusion(f32[128,128,128]{2,1,0:T(8,128)} %fusion, f32[128,128,128]{2,1,0:T(8,128)} %fusion.4, bf16[1,1,128,128,128]{4,3,2,1,0:T(8,128)(2,1)} %param.13, f32[128,128,128]{2,1,0:T(8,128)} %gather_fusion.1, pred[128]{0:T(512)(128)(4,1)S(1)} %get-tuple-element.6), kind=kOutput, calls=%fused_computation.11 | convolution fusion | flops 557842432 | bytes 37748864 | tf_op jit(solution)/shard_map/tji,tjf->tif/dot_general | solution.py:36
  449.3 9.4 %copy.17 = f32[128,128,128]{0,2,1:T(8,128)} copy(f32[128,128,128]{1,2,0:T(8,128)} %add_bitcast_fusion) | data formatting | bytes 16777216 | tf_op jit(solution)/shard_map/add | solution.py:37
  458.7 0.0 copy-start.4
  458.7 3.8 bitcast_convert_fusion
  462.5 2.0 copy-done.4
  464.5 1.9 subtract_convert_fusion
  466.4 1.2 fusion.43
  467.6 1.2 convolution_add_fusion.3
  468.8 0.0 copy-start.1
  468.8 0.0 copy-start.6
  468.8 1.2 convolution_add_fusion.2
  470.0 1.1 reshape.219
  471.2 0.0 reduce-scatter.5.cloned.1.call-update
  471.2 0.0 all-reduce.2.cloned.1.call-start
  471.2 76.1 %psum.15 = f32[256]{0:T(256)} all-reduce(f32[256]{0:T(256)S(1)} %get-tuple-element.4), channel_id=1, replica_groups=mesh['row'=8,'col'=32] {'row','col'}, use_global_device_ids=true, to_apply=%region_4.5 | all-reduce | flops 256 | bytes 2048 | tf_op jit(solution)/shard_map/psum | solution.py:77
  547.4 0.0 copy-done.6
  547.4 1.1 fusion.28
  548.5 0.0 all-reduce.2.cloned.1.call-update
  548.5 0.0 reduce-scatter.5.cloned.1.call-done
  548.5 1.6 multiply_convert_fusion.1
  550.2 234.2 %all-reduce.2.cloned.1.call-done = f32[128,256]{1,0:T(8,128)} async-done(((f32[128,256]{1,0:T(8,128)}), f32[128,256]{1,0:T(8,128)}) %all-reduce.2.cloned.1.call-update) | async-done | bytes 131088 | tf_op jit(solution)/shard_map/psum | solution.py:77
  784.4 1.6 copy.24
  785.9 0.0 copy-done.1
  (2 shorter events, 0.0 us)
Async XLA Ops:
  7.2 276.3 %copy-start = (bf16[128,256]{1,0:T(8,128)(2,1)S(1)}, bf16[128,256]{1,0:T(8,128)(2,1)}, u32[]{:S(2)}) copy-start(bf16[128,256]{1,0:T(8,128)(2,1)} %param.9) | copy-start | bytes 196612
  7.2 276.3 %reduce-scatter.3.cloned.1.call-start = ((), (), s32[]{:S(2)}) async-start(), calls=%async_computation.2 | async-start | bytes 4325376 | tf_op jit(solution)/shard_map/reduce_scatter | solution.py:63
  50.9 5.8 copy-start.3
  70.2 213.3 %copy-start.7 = (bf16[256,256]{1,0:T(8,128)(2,1)S(1)}, bf16[256,256]{1,0:T(8,128)(2,1)}, u32[]{:S(2)}) copy-start(bf16[256,256]{1,0:T(8,128)(2,1)} %param.11) | copy-start | bytes 393220
  70.2 213.3 %copy-start.8 = (f32[256]{0:T(256)S(1)}, f32[256]{0:T(256)}, u32[]{:S(2)}) copy-start(f32[256]{0:T(256)} %param.10) | copy-start | bytes 3076
  70.2 341.3 %all-gather.2.cloned.1.call-start = ((), (), s32[]{:S(2)}) async-start(), calls=%async_computation.3 | async-start | bytes 4325376 | tf_op jit(solution)/shard_map/all_gather | solution.py:71
  286.4 262.1 %reduce-scatter.5.cloned.1.call-start = ((), (), s32[]{:S(2)}) async-start(), calls=%async_computation.4 | async-start | bytes 1179648 | tf_op jit(solution)/shard_map/reduce_scatter | solution.py:75
  418.0 10.4 %copy-start.2 = (f32[128,128,128]{2,1,0:T(8,128)S(1)}, f32[128,128,128]{2,1,0:T(8,128)}, u32[]{:S(2)}) copy-start(f32[128,128,128]{2,1,0:T(8,128)} %gather_fusion.1) | copy-start | bytes 25165828
  418.0 10.4 %copy-start.5 = (bf16[1,1,128,128,128]{4,3,2,1,0:T(8,128)(2,1)S(1)}, bf16[1,1,128,128,128]{4,3,2,1,0:T(8,128)(2,1)}, u32[]{:S(2)}) copy-start(bf16[1,1,128,128,128]{4,3,2,1,0:T(8,128)(2,1)} %param.13) | copy-start | bytes 12582916
  458.7 5.8 copy-start.4
  468.8 317.1 %copy-start.1 = (bf16[128,256]{1,0:T(8,128)(2,1)S(1)}, bf16[128,256]{1,0:T(8,128)(2,1)}, u32[]{:S(2)}) copy-start(bf16[128,256]{1,0:T(8,128)(2,1)} %param.9) | copy-start | bytes 196612
  468.8 78.6 %copy-start.6 = (f32[256,128]{1,0:T(8,128)S(1)}, f32[256,128]{1,0:T(8,128)}, u32[]{:S(2)}) copy-start(f32[256,128]{1,0:T(8,128)} %reduce-scatter.3.cloned.1.call-done) | copy-start | bytes 393220
  471.2 313.2 %all-reduce.2.cloned.1.call-start = ((), (), s32[]{:S(2)}) async-start(), calls=%async_computation.5 | async-start | bytes 262144 | tf_op jit(solution)/shard_map/psum | solution.py:77
Sparse Core Ops, SparseCore 0:
  70.4 213.0 reduce-scatter.2
  287.6 123.9 all-gather.1
  471.3 32.8 reduce-scatter.4
  548.6 235.6 all-reduce.1
where the time goes:
time: 793 us; the launch traced here: 792 us
  waiting for transfers between devices  572 us (72%)
  blocking collectives  93.9 us (12%)
  matrix products  55.5 us (7%)
  local copies, waits for them, and re-layouts  39.9 us (5%)
  other arithmetic  16 us (2%)
  between operations  14.5 us (2%)
    psum x1, waiting for transfers between devices, per_device(): lax.psum((weight_term, jnp.sum(grad_pre, axis=0)), ('row', 'col'))  234 us
    reduce_scatter x1, waiting for transfers between devices, per_device(): lax.psum_scatter(partial_value, 'col', scatter_dimension=0, tiled=True)  213 us
    all_gather x1, waiting for transfers between devices, per_device(): gathered_back = lax.all_gather(outgoing, 'col', axis=0, tiled=True)  125 us
    psum x1, blocking collectives, per_device(): lax.psum((weight_term, jnp.sum(grad_pre, axis=0)), ('row', 'col'))  76.1 us
    all_gather x1, blocking collectives, per_device(): gathered = lax.all_gather(scaled, 'row', axis=0, tiled=True)  17.8 us
  transfers between devices with their start and end apart: 4, of which 3 were waited for; matrix products, arithmetic and copies ran while one was open for 0% of the time, Pallas kernels for 0%

commit v1 on v0

v1 whole, which is shorter than its diff:
```python
import jax
import jax.numpy as jnp
from jax import lax
from jax.experimental import pallas as pl
from jax.experimental.pallas import tpu as pltpu
from jax.sharding import PartitionSpec as P

MESH = pl.DeviceIdType.MESH
F32 = jnp.float32
BF16 = jnp.bfloat16
I32 = jnp.int32
UNROLL = 8
MAX_COPIES = 192


def two_parts(values):
    upper = values.astype(BF16)
    return upper, (values - upper.astype(F32)).astype(BF16)


def dot(a, b):
    return jnp.dot(a, b, preferred_element_type=F32)


def dot_general(a, b, dims):
    return lax.dot_general(a, b, (dims, ((), ())), preferred_element_type=F32)


def segment_plan(key, shift, eye, lane2, sub2, slots):
    key_col = jnp.sum(jnp.where(eye, key.astype(F32), 0.0), axis=1, keepdims=True).astype(I32)
    less = key < key_col
    rank = jnp.sum(jnp.where(less, 1.0, 0.0), axis=1, keepdims=True).astype(I32)
    seg_col = key_col >> shift
    before = jnp.where(less, 1.0, 0.0) * jnp.where((key >> shift) == seg_col, 1.0, 0.0)
    same = jnp.max(before, axis=1, keepdims=True)
    perm = rank == lane2

    def permuted(column):
        return jnp.sum(jnp.where(perm, column, 0.0), axis=0, keepdims=True).astype(I32)

    order = permuted(sub2.astype(F32))
    sorted_key = permuted(key_col.astype(F32))
    sorted_same = permuted(same)
    upto = jnp.sum(jnp.where(seg_col <= lane2, 1.0, 0.0), axis=0, keepdims=True).astype(I32)
    here = jnp.sum(jnp.where(seg_col == lane2, 1.0, 0.0), axis=0, keepdims=True).astype(I32)
    last = jnp.where(here > 0, upto - 1, slots)
    return order, sorted_key, sorted_same, last


def layer_kernel(
    feat_ref, weight_hbm, bias_ref, cot_hbm, deg_ref, tiles_hbm, pos_ref, cnt_ref,
    act_ref, gf_ref, gw_ref, gb_ref,
    tiles, weight_v, cot_v, table_v, table, gathered, run, part, transit, landed, quarter, own_small,
    transit_q, landed_q, halves, z_send, z_recv, grads, hid_v, pre_v, back, back_in, back_sum, back_recv,
    gw_part, gw_in, gw_x, gw_y, gw_z, gw_all, local_sem, send_sem, recv_sem,
):
    slots, blk, _ = tiles.shape
    row = lax.axis_index("row")
    col = lax.axis_index("col")
    core = lax.rem(row, 2)
    zl = row // 2
    x = col // 8
    zh = lax.rem(col // 4, 2)
    y = lax.rem(col, 4)

    def step4(v, d):
        return lax.rem(v + d, 4)

    def at_x(d):
        return (row, step4(x, d) * 8 + zh * 4 + y)

    def at_y(d):
        return (row, x * 8 + zh * 4 + step4(y, d))

    def at_row(other):
        return (other, col)

    z_peer = (row, x * 8 + (1 - zh) * 4 + y)
    sibling = at_row(zl * 2 + 1 - core)

    barrier = pltpu.get_barrier_semaphore()
    peers = [at_x(d) for d in (1, 2, 3)] + [at_y(d) for d in (1, 2, 3)] + [z_peer]
    peers += [at_row(lax.rem(row + d, 8)) for d in range(1, 8)]
    for peer in peers:
        pl.semaphore_signal(barrier, inc=1, device_id=peer, device_id_type=MESH)

    tiles_copy = pltpu.make_async_copy(tiles_hbm, tiles, local_sem.at[0])
    tiles_copy.start()
    weight_copy = pltpu.make_async_copy(weight_hbm, weight_v, local_sem.at[1])
    weight_copy.start()
    cot_copy = pltpu.make_async_copy(cot_hbm, cot_v, local_sem.at[2])
    cot_copy.start()

    eye_b = lax.broadcasted_iota(I32, (blk, blk), 0) == lax.broadcasted_iota(I32, (blk, blk), 1)
    scale_row = [lax.rsqrt(deg_ref[pl.ds(b, 1), :].astype(F32)) for b in range(2)]
    scale_col = [jnp.sum(jnp.where(eye_b, s, 0.0), axis=1, keepdims=True) for s in scale_row]
    for b in range(2):
        rows = pl.ds(b * blk, blk)
        gathered[row * 2 + b] = (scale_col[b] * feat_ref[rows, :].astype(F32)).astype(BF16)

    pl.semaphore_wait(barrier, len(peers))

    started = []

    def send(src, dst, device):
        n = len(started)
        copy = pltpu.make_async_remote_copy(
            src_ref=src, dst_ref=dst, send_sem=send_sem.at[n], recv_sem=recv_sem.at[n],
            device_id=device, device_id_type=MESH,
        )
        copy.start()
        started.append(copy)
        return copy

    def own_pair(r):
        return gathered.at[pl.ds(r * 2, 2)]

    far = [send(own_pair(row), own_pair(row), at_row(step4(zl, d) * 2 + core)) for d in (1, 2, 3)]
    near = [send(own_pair(row), own_pair(row), sibling)]

    pos = pos_ref[...]
    lane = lax.broadcasted_iota(I32, (1, slots), 1)
    live = lane < cnt_ref[0, 0]
    lane2 = lax.broadcasted_iota(I32, (slots, slots), 1)
    sub2 = lax.broadcasted_iota(I32, (slots, slots), 0)
    eye = lane2 == sub2
    key_f = jnp.where(live, pos, 1024 + lane)
    key_b = jnp.where(live, (pos & 15) * 64 + (pos >> 4), 1024 + lane)
    order_f, sorted_f, same_f, last_f = segment_plan(key_f, 4, eye, lane2, sub2, slots)
    order_b, sorted_b, same_b, last_b = segment_plan(key_b, 6, eye, lane2, sub2, slots)
    rb = sorted_b & 63
    rb_x, rb_z, rb_y = rb >> 4, (rb >> 3) & 1, (rb >> 1) & 3
    slot_b = jnp.where((rb & 1) == 0, (rb_y * 4 + rb_x) * 2 + rb_z, 32 + (rb_x * 4 + rb_y) * 2 + rb_z)
    for n, line in enumerate((order_f, sorted_f & 15, same_f, last_f, order_b, slot_b, same_b, last_b)):
        table_v[pl.ds(n, 1), :] = line
    table_copy = pltpu.make_async_copy(table_v, table, local_sem.at[3])
    table_copy.start()
    run[slots] = jnp.zeros((blk, run.shape[2]), BF16)
    table_copy.wait()
    tiles_copy.wait()

    for d in (1, 2, 3):
        far[d - 1].wait_recv()
        other = step4(zl, 4 - d) * 2 + core
        near.append(send(own_pair(other), own_pair(other), sibling))
    for copy in near:
        copy.wait_recv()

    def forward(g, acc):
        steps = [g * UNROLL + u for u in range(UNROLL)]
        terms = [dot(tiles[table[0, p] & (slots - 1)], gathered[table[1, p] & 15]) for p in steps]
        for p, term in zip(steps, terms):
            acc = acc * table[2, p].astype(F32) + term
            run[p] = acc.astype(BF16)
        return acc

    zero = jnp.zeros((blk, run.shape[2]), F32)
    lax.fori_loop(0, slots // UNROLL, forward, zero)

    def ending(line, segment):
        return jnp.clip(table[line, segment], 0, slots)

    def place(c, carry):
        cx, cz, cy = c // 8, lax.rem(c // 4, 2), lax.rem(c, 4)
        part[0, cy, cx, cz] = run[ending(3, c * 2)]
        part[1, cx, cy, cz] = run[ending(3, c * 2 + 1)]
        return carry

    lax.fori_loop(0, 32, place, 0)

    big, small = (y, x), (x, y)
    at_big, at_small = (at_y, at_x), (at_x, at_y)
    offsets = (2, 1, 3, 0)
    copies = {}

    def issue(h, n):
        q = step4(small[h], offsets[n])
        opp, right, left = (step4(big[h], d) for d in (2, 1, 3))
        up, down = at_big[h](1), at_big[h](3)
        copies[h, n] = [
            send(part.at[h, opp, q, 0], transit.at[h, n, 0], up),
            send(part.at[h, opp, q, 1], transit.at[h, n, 1], down),
            send(part.at[h, right, q, 1], landed.at[h, n, 0, 1], up),
            send(part.at[h, left, q, 0], landed.at[h, n, 1, 0], down),
        ]

    def combine(h, n):
        q = step4(small[h], offsets[n])
        right, left = step4(big[h], 1), step4(big[h], 3)
        c = copies[h, n]
        c[0].wait_recv()
        part[h, right, q, 0] = (part[h, right, q, 0].astype(F32) + transit[h, n, 0].astype(F32)).astype(BF16)
        c.append(send(part.at[h, right, q, 0], landed.at[h, n, 0, 0], at_big[h](1)))
        c[1].wait_recv()
        part[h, left, q, 1] = (part[h, left, q, 1].astype(F32) + transit[h, n, 1].astype(F32)).astype(BF16)
        c.append(send(part.at[h, left, q, 1], landed.at[h, n, 1, 1], at_big[h](3)))

    def finish(h, n):
        q = step4(small[h], offsets[n])
        for c in copies[h, n][2:]:
            c.wait_recv()
        for z in range(2):
            total = (
                part[h, big[h], q, z].astype(F32)
                + landed[h, n, 0, z].astype(F32)
                + landed[h, n, 1, z].astype(F32)
            )
            if n < 3:
                quarter[h, n, z] = total.astype(BF16)
            else:
                own_small[h, z] = total

    def small_first(h):
        copies[h, "s"] = [
            send(quarter.at[h, 0, 0], transit_q.at[h, 0], at_small[h](1)),
            send(quarter.at[h, 0, 1], transit_q.at[h, 1], at_small[h](3)),
        ]

    def small_up(h):
        c = copies[h, "s"]
        c.append(send(quarter.at[h, 1, 1], landed_q.at[h, 0, 1], at_small[h](1)))
        c[0].wait_recv()
        quarter[h, 1, 0] = (quarter[h, 1, 0].astype(F32) + transit_q[h, 0].astype(F32)).astype(BF16)
        c.append(send(quarter.at[h, 1, 0], landed_q.at[h, 0, 0], at_small[h](1)))

    def small_down(h):
        c = copies[h, "s"]
        c.append(send(quarter.at[h, 2, 0], landed_q.at[h, 1, 0], at_small[h](3)))
        c[1].wait_recv()
        quarter[h, 2, 1] = (quarter[h, 2, 1].astype(F32) + transit_q[h, 1].astype(F32)).astype(BF16)
        c.append(send(quarter.at[h, 2, 1], landed_q.at[h, 1, 1], at_small[h](3)))

    def small_finish(h):
        for c in copies[h, "s"][2:]:
            c.wait_recv()
        for z in range(2):
            halves[h, z] = (
                own_small[h, z] + landed_q[h, 0, z].astype(F32) + landed_q[h, 1, z].astype(F32)
            )
        z_send[h] = halves[h, 1 - zh].astype(BF16)
        copies[h, "z"] = send(z_send.at[h], z_recv.at[h], z_peer)

    both = (0, 1)
    for n in (0, 1):
        for h in both:
            issue(h, n)
    for h in both:
        combine(h, 0)
    for h in both:
        issue(h, 2)
    for h in both:
        combine(h, 1)
    for h in both:
        issue(h, 3)
    for h in both:
        finish(h, 0)
        small_first(h)
    for h in both:
        combine(h, 2)
    for h in both:
        finish(h, 1)
        small_up(h)
    for h in both:
        combine(h, 3)
    for h in both:
        finish(h, 2)
        small_down(h)
    for h in both:
        finish(h, 3)
    for h in both:
        small_finish(h)

    weight_copy.wait()
    cot_copy.wait()
    weight = weight_v[...]
    bias = bias_ref[...]
    first, second = zh, 1 - zh

    def spread(h, cs, z, key, both_ways=True):
        ref = grads.at[h, big[h], cs, z]
        copies[h, "b", key] = (send(ref, ref, at_big[h](1)), send(ref, ref, at_big[h](3)))

    def spread_small(h, z, key):
        ref = grads.at[h, big[h], small[h], z]
        copies[h, "p", key] = (send(ref, ref, at_small[h](1)), send(ref, ref, at_small[h](3)))

    for h in both:
        copies[h, "z"].wait_recv()
        hidden = scale_col[h] * (halves[h, zh] + z_recv[h].astype(F32))
        upper, lower = two_parts(hidden)
        preact = dot(upper, weight) + dot(lower, weight) + bias
        gate = 1.0 / (1.0 + jnp.exp(-preact))
        rows = pl.ds(h * blk, blk)
        act_ref[rows, :] = (preact * gate).astype(BF16)
        grad_pre = cot_v[rows, :].astype(F32) * gate * (1.0 + preact * (1.0 - gate))
        hid_v[h] = hidden
        pre_v[h] = grad_pre
        upper, lower = two_parts(grad_pre)
        nt = ((1,), (1,))
        outgoing = scale_row[h] * (dot_general(weight, upper, nt) + dot_general(weight, lower, nt))
        grads[h, big[h], small[h], first] = outgoing.astype(BF16)
        ref = grads.at[h, big[h], small[h], first]
        copies[h, "g"] = send(ref, ref, z_peer)
        spread_small(h, first, "a")
        spread(h, small[h], first, (0, "a"))

    total = None
    bias_sum = None
    tn = ((0,), (0,))
    for h in both:
        hu, hl = two_parts(hid_v[h])
        gu, gl = two_parts(pre_v[h])
        term = dot_general(hu, gu, tn) + dot_general(hu, gl, tn) + dot_general(hl, gu, tn)
        sums = jnp.sum(pre_v[h], axis=0, keepdims=True)
        total = term if total is None else total + term
        bias_sum = sums if bias_sum is None else bias_sum + sums
    share = total.shape[0] // 8
    for r in range(8):
        gw_part[r, pl.ds(0, share), :] = total[r * share:(r + 1) * share, :]
        gw_part[r, pl.ds(share, 8), :] = jnp.broadcast_to(bias_sum, (8, bias_sum.shape[1]))
    gw1 = []
    for d in range(1, 8):
        other = lax.rem(row + d, 8)
        gw1.append(send(gw_part.at[other], gw_in.at[d - 1], at_row(other)))

    for h in both:
        copies[h, "g"].wait_recv()
        spread_small(h, second, "b")
        spread(h, small[h], second, (0, "b"))

    def forward_small(h, key):
        up, down = copies[h, "p", key]
        z = first if key == "a" else second
        left, right = step4(small[h], 3), step4(small[h], 1)
        if key == "a":
            up.wait_recv()
            ref = grads.at[h, big[h], left, z]
            copies[h, "f", key] = send(ref, ref, at_small[h](1))
            spread(h, left, z, (3, key))
            down.wait_recv()
            spread(h, right, z, (1, key))
        else:
            down.wait_recv()
            ref = grads.at[h, big[h], right, z]
            copies[h, "f", key] = send(ref, ref, at_small[h](3))
            spread(h, right, z, (1, key))
            up.wait_recv()
            spread(h, left, z, (3, key))

    def forward_big(h, off, key):
        up, down = copies[h, "b", (off, key)]
        cs = step4(small[h], off)
        if key == "a":
            up.wait_recv()
            ref = grads.at[h, step4(big[h], 3), cs, first]
            copies[h, "w", (off, key)] = send(ref, ref, at_big[h](1))
        else:
            down.wait_recv()
            ref = grads.at[h, step4(big[h], 1), cs, second]
            copies[h, "w", (off, key)] = send(ref, ref, at_big[h](3))

    def finish_big(h, off, key):
        up, down = copies[h, "b", (off, key)]
        (down if key == "a" else up).wait_recv()
        copies[h, "w", (off, key)].wait_recv()

    for key in ("a", "b"):
        for h in both:
            forward_small(h, key)
        for h in both:
            forward_big(h, 0, key)
    for key in ("a", "b"):
        for h in both:
            copies[h, "f", key].wait_recv()
            spread(h, step4(small[h], 2), first if key == "a" else second, (2, key))
        for h in both:
            forward_big(h, 3, key)
            forward_big(h, 1, key)

    for copy in gw1:
        copy.wait_recv()
    piece = gw_part[row]
    for d in range(7):
        piece = piece + gw_in[d]
    gw_x[x] = piece
    gw2 = [send(gw_x.at[x], gw_x.at[x], at_x(d)) for d in (1, 2, 3)]

    for key in ("a", "b"):
        for h in both:
            forward_big(h, 2, key)
    for off in (0, 1, 3, 2):
        for key in ("a", "b"):
            for h in both:
                finish_big(h, off, key)

    for copy in gw2:
        copy.wait_recv()
    gw_y[y] = gw_x[0] + gw_x[1] + gw_x[2] + gw_x[3]
    gw3 = [send(gw_y.at[y], gw_y.at[y], at_y(d)) for d in (1, 2, 3)]

    def backward(g, acc):
        steps = [g * UNROLL + u for u in range(UNROLL)]
        terms = [dot(flat_grad(table[5, p] & 63), tiles[table[4, p] & (slots - 1)]) for p in steps]
        for p, term in zip(steps, terms):
            acc = acc * table[6, p].astype(F32) + term
            run[p] = acc.astype(BF16)
        return acc

    def flat_grad(s):
        return grads[s // 32, lax.rem(s // 8, 4), lax.rem(s // 2, 4), lax.rem(s, 2)]

    zero_t = jnp.zeros((run.shape[1], blk), F32)
    mid = slots // UNROLL // 2
    acc = lax.fori_loop(0, mid, backward, zero_t)
    for copy in gw3:
        copy.wait_recv()
    gw_z[zh] = gw_y[0] + gw_y[1] + gw_y[2] + gw_y[3]
    gw4 = send(gw_z.at[zh], gw_z.at[zh], z_peer)
    lax.fori_loop(mid, slots // UNROLL, backward, acc)

    def place_back(r, carry):
        for b in range(2):
            back[lax.rem(r, 2), r // 2, b] = run[ending(7, r * 2 + b)]
        return carry

    lax.fori_loop(0, 8, place_back, 0)

    near = []
    for d in (1, 2, 3, 0):
        other = step4(zl, d)
        near.append(send(back.at[1 - core, other], back_in.at[d], sibling))
    gw4.wait_recv()
    gw_all[row] = gw_z[0] + gw_z[1]
    gw5 = [send(gw_all.at[row], gw_all.at[row], at_row(lax.rem(row + d, 8))) for d in range(1, 8)]
    far = []
    for n, d in enumerate((1, 2, 3)):
        other = step4(zl, d)
        near[n].wait_recv()
        back_sum[n] = (back[core, other].astype(F32) + back_in[d].astype(F32)).astype(BF16)
        far.append(send(back_sum.at[n], back_recv.at[n], at_row(other * 2 + core)))
    near[3].wait_recv()
    own = back[core, zl].astype(F32) + back_in[0].astype(F32)
    for copy in gw5:
        copy.wait_recv()
    for r in range(8):
        gw_ref[pl.ds(r * share, share), :] = gw_all[r, pl.ds(0, share), :]
    gb_ref[...] = gw_all[0, pl.ds(share, 1), :]
    for n in range(3):
        far[n].wait_recv()
        own = own + back_recv[n].astype(F32)
    for b in range(2):
        gf_ref[pl.ds(b * blk, blk), :] = jnp.transpose(scale_row[b] * own[b]).astype(BF16)

    assert len(started) <= MAX_COPIES
    for copy in started:
        copy.wait_send()


def per_device(
    features, weight, bias_vector, cotangent, degrees, adjacency_tiles, tile_positions, tile_counts
):
    slots, blk = adjacency_tiles.shape[2:4]
    f_in, hid = weight.shape
    nodes = features.shape[0]
    share = f_in // 8
    vmem = pl.BlockSpec(memory_space=pltpu.VMEM)
    anywhere = pl.BlockSpec(memory_space=pl.ANY)
    piece = (share + 8, hid)
    outs = pl.pallas_call(
        layer_kernel,
        out_shape=(
            jax.ShapeDtypeStruct((nodes, hid), BF16),
            jax.ShapeDtypeStruct((nodes, f_in), BF16),
            jax.ShapeDtypeStruct((f_in, hid), F32),
            jax.ShapeDtypeStruct((1, hid), F32),
        ),
        in_specs=[
            vmem, anywhere, vmem, anywhere, vmem, anywhere, vmem, pl.BlockSpec(memory_space=pltpu.SMEM),
        ],
        out_specs=(vmem, vmem, vmem, vmem),
        scratch_shapes=[
            pltpu.VMEM((slots, blk, blk), BF16),
            pltpu.VMEM((f_in, hid), BF16),
            pltpu.VMEM((nodes, hid), BF16),
            pltpu.VMEM((8, slots), I32),
            pltpu.SMEM((8, slots), I32),
            pltpu.VMEM((16, blk, f_in), BF16),
            pltpu.VMEM((slots + 1, blk, f_in), BF16),
            pltpu.VMEM((2, 4, 4, 2, blk, f_in), BF16),
            pltpu.VMEM((2, 4, 2, blk, f_in), BF16),
            pltpu.VMEM((2, 4, 2, 2, blk, f_in), BF16),
            pltpu.VMEM((2, 3, 2, blk, f_in), BF16),
            pltpu.VMEM((2, 2, blk, f_in), F32),
            pltpu.VMEM((2, 2, blk, f_in), BF16),
            pltpu.VMEM((2, 2, 2, blk, f_in), BF16),
            pltpu.VMEM((2, 2, blk, f_in), F32),
            pltpu.VMEM((2, blk, f_in), BF16),
            pltpu.VMEM((2, blk, f_in), BF16),
            pltpu.VMEM((2, 4, 4, 2, f_in, blk), BF16),
            pltpu.VMEM((2, blk, f_in), F32),
            pltpu.VMEM((2, blk, hid), F32),
            pltpu.VMEM((2, 4, 2, f_in, blk), BF16),
            pltpu.VMEM((4, 2, f_in, blk), BF16),
            pltpu.VMEM((3, 2, f_in, blk), BF16),
            pltpu.VMEM((3, 2, f_in, blk), BF16),
            pltpu.VMEM((8,) + piece, F32),
            pltpu.VMEM((7,) + piece, F32),
            pltpu.VMEM((4,) + piece, F32),
            pltpu.VMEM((4,) + piece, F32),
            pltpu.VMEM((2,) + piece, F32),
            pltpu.VMEM((8,) + piece, F32),
            pltpu.SemaphoreType.DMA((4,)),
            pltpu.SemaphoreType.DMA((MAX_COPIES,)),
            pltpu.SemaphoreType.DMA((MAX_COPIES,)),
        ],
        compiler_params=pltpu.CompilerParams(
            collective_id=0, has_side_effects=True, vmem_limit_bytes=40 * 1024 * 1024
        ),
        name="graph_layer",
    )(
        features,
        weight,
        bias_vector.reshape(1, hid),
        cotangent,
        degrees.reshape(2, blk),
        adjacency_tiles.reshape(slots, blk, blk),
        tile_positions.reshape(1, slots),
        tile_counts,
    )
    activations, grad_features, grad_weight, grad_bias = outs
    return activations, grad_features, grad_weight, grad_bias.reshape(hid)


def solution(mesh):
    placed = (
        P(("row", "col"), None),
        P(),
        P(),
        P(("row", "col"), None),
        P(("row", "col")),
        P("row", "col", None, None, None),
        P("row", "col", None),
        P("row", "col"),
    )
    return jax.shard_map(
        per_device,
        mesh=mesh,
        in_specs=placed,
        out_specs=(P(("row", "col"), None), P(("row", "col"), None), P(), P()),
        check_vma=False,
    )
```

time: 793 us -> 93.2 us (0.12)
  waiting for transfers between devices: 572 us -> 0 us
  blocking collectives: 93.9 us -> 0 us
  Pallas kernels: 0 us -> 81.2 us
  matrix products: 55.5 us -> 0 us
  local copies, waits for them, and re-layouts: 39.9 us -> 9.28 us
  other arithmetic: 16 us -> 0 us
  between operations: 14.5 us -> 1.3 us
    psum x1 -> x0, waiting for transfers between devices: 234 us -> none  [per_device(): lax.psum((weight_term, jnp.sum(grad_pre, axis=0)), ('row', 'col'))]
    reduce_scatter x2 -> x0, waiting for transfers between devices: 213 us -> none  [the longest x1 213 us: per_device(): lax.psum_scatter(partial_value, 'col', scatter_dimension=0, tiled=True)]
    all_gather x1 -> x0, waiting for transfers between devices: 125 us -> none  [per_device(): gathered_back = lax.all_gather(outgoing, 'col', axis=0, tiled=True)]
    pallas_call x0 -> x1, Pallas kernels: none -> 81.2 us  [per_device(): pl.pallas_call(layer_kernel, out_shape=(jax.ShapeDtypeStruct((nodes, hid)...]
    psum x1 -> x0, blocking collectives: 76.1 us -> none  [per_device(): lax.psum((weight_term, jnp.sum(grad_pre, axis=0)), ('row', 'col'))]
    dot_general x13 -> x0, matrix products: 55.5 us -> none  [the longest x1 15.1 us: tile_product(): jnp.einsum(form, tile_data, pieces[2], preferred_element_type=jnp.float32)]
    all_gather x1 -> x0, blocking collectives: 17.8 us -> none  [per_device(): gathered = lax.all_gather(scaled, 'row', axis=0, tiled=True)]
    convert_element_type x6 -> x0, other arithmetic: 14 us -> none  [the longest x2 7.64 us: split_three(): upper = values.astype(jnp.bfloat16)]
  transfers between devices with their start and end apart: 4 -> 0, of which waited for: 3 -> 0; matrix products, arithmetic and copies ran while one was open for 0% -> 0% of each run, Pallas kernels for 0% -> 0%
where the time goes in v1:
time: 93.2 us; the launch traced here: 91.7 us
  Pallas kernels  81.2 us (87%)
  local copies, waits for them, and re-layouts  9.28 us (10%)
  between operations  1.3 us (1%)
    pallas_call x1, Pallas kernels, per_device(): pl.pallas_call(layer_kernel, out_shape=(jax.ShapeDtypeStruct((nodes, hid)...  81.2 us
    unnamed x18, local copies, waits for them, and re-layouts  9.28 us

profile of v1, /device:TPU:1, one launch (start us, length us, event | category | flops | bytes accessed | tf_op | source)
XLA Modules:
  0.0 91.7 jit_solution(5223292917965275902)
XLA Ops:
  1.3 0.0 copy-start
  1.3 2.2 %copy-done = bf16[1,1,128,128,128]{4,3,2,1,0:T(8,128)(2,1)S(1)} copy-done((bf16[1,1,128,128,128]{4,3,2,1,0:T(8,128)(2,1)S(1)}, bf16[1,1,128,128,128]{4,3,2,1,0:T(8,128)(2,1)}, u32[]{:S(2)}) %copy-start) | copy-done | bytes 4194328
  3.5 0.0 copy-start.1
  3.5 0.9 copy-done.1
  4.4 0.0 copy-start.2
  4.4 0.8 copy-done.2
  5.2 0.0 copy-start.3
  5.2 0.8 copy-done.3
  6.1 0.0 copy-start.4
  6.1 0.7 copy-done.4
  6.7 0.0 copy-start.5
  6.7 0.7 copy-done.5
  7.4 0.0 copy-start.6
  7.4 0.7 copy-done.6
  8.1 81.2 %graph_layer.1 = (bf16[256,256]{1,0:T(8,128)(2,1)S(1)}, bf16[256,128]{1,0:T(8,128)(2,1)S(1)}, f32[128,256]{1,0:T(8,128)S(1)}, f32[1,256]{1,0:T(1,128)S(1)}) custom-call(bf16[256,128]{1,0:T(8,128)(2,1)S(1)} %copy-done.2, bf16[128,256]{1,0:T(8,128)(2,1)S(1)} %copy-done.3, f32[1,256]{1,0:T(1,128)S(1)} %bitcast.6, bf16[256,256]{1,0:T(8,128)(2,1)S(1)} %copy-done.1, ...), custom_call_target="tpu_custom_call" | custom-call | tf_op jit(solution)/shard_map/graph_layer/pallas_call | solution.py:469
  89.2 0.7 copy.17
  89.9 0.6 copy.18
  90.5 0.7 copy.19
  91.2 0.6 copy.20
Async XLA Ops:
  1.3 2.2 %copy-start = (bf16[1,1,128,128,128]{4,3,2,1,0:T(8,128)(2,1)S(1)}, bf16[1,1,128,128,128]{4,3,2,1,0:T(8,128)(2,1)}, u32[]{:S(2)}) copy-start(bf16[1,1,128,128,128]{4,3,2,1,0:T(8,128)(2,1)} %param.13) | copy-start | bytes 12582916
  3.5 0.9 copy-start.1
  4.4 0.8 copy-start.2
  5.2 0.8 copy-start.3
  6.1 0.7 copy-start.4
  6.7 0.7 copy-start.5
  7.4 0.7 copy-start.6

commit v2 on v1

v2 whole, which is shorter than its diff:
```python
import jax
import jax.numpy as jnp
from jax import lax
from jax.experimental import pallas as pl
from jax.experimental.pallas import tpu as pltpu
from jax.sharding import PartitionSpec as P

MESH = pl.DeviceIdType.MESH
F32 = jnp.float32
BF16 = jnp.bfloat16
I32 = jnp.int32
UNROLL = 32
MAX_COPIES = 192
OFFSETS = (2, 1, 3, 0)
VMEM_BYTES = 60 * 1024 * 1024


def two_parts(values):
    upper = values.astype(BF16)
    return upper, (values - upper.astype(F32)).astype(BF16)


def dot(a, b):
    return jnp.dot(a, b, preferred_element_type=F32)


def dot_general(a, b, dims):
    return lax.dot_general(a, b, (dims, ((), ())), preferred_element_type=F32)


def segment_plan(key, shift, eye, lane2, sub2, slots):
    key_col = jnp.sum(jnp.where(eye, key.astype(F32), 0.0), axis=1, keepdims=True).astype(I32)
    less = key < key_col
    rank = jnp.sum(jnp.where(less, 1.0, 0.0), axis=1, keepdims=True).astype(I32)
    seg_col = key_col >> shift
    before = jnp.where(less, 1.0, 0.0) * jnp.where((key >> shift) == seg_col, 1.0, 0.0)
    same = jnp.max(before, axis=1, keepdims=True)
    perm = rank == lane2

    def permuted(column):
        return jnp.sum(jnp.where(perm, column, 0.0), axis=0, keepdims=True).astype(I32)

    order = permuted(sub2.astype(F32))
    sorted_key = permuted(key_col.astype(F32))
    sorted_same = permuted(same)
    upto = jnp.sum(jnp.where(seg_col <= lane2, 1.0, 0.0), axis=0, keepdims=True).astype(I32)
    here = jnp.sum(jnp.where(seg_col == lane2, 1.0, 0.0), axis=0, keepdims=True).astype(I32)
    last = jnp.where(here > 0, upto - 1, slots)
    return order, sorted_key, sorted_same, last


def layer_kernel(
    feat_hbm, weight_hbm, bias_hbm, cot_hbm, deg_hbm, tiles_hbm, pos_hbm, cnt_hbm,
    act_hbm, gf_hbm, gw_hbm, gb_hbm,
    feat_ref, bias_ref, deg_ref, pos_ref, cnt_ref, act_ref, gf_ref, gw_ref, gb_ref,
    tiles, weight_v, cot_v, table_v, table, gathered, run, part, landed, quarter, own_small,
    landed_q, halves, z_send, z_recv, grads, hid_v, pre_v, back, back_in, back_sum, back_recv,
    gw_part, gw_in, gw_sum, gw_row, gw_x, gw_y, gw_z, gw_all, local_sem, send_sem, recv_sem,
):
    slots, blk, _ = tiles.shape
    row = lax.axis_index("row")
    col = lax.axis_index("col")
    core = lax.rem(row, 2)
    zl = row // 2
    x = col // 8
    zh = lax.rem(col // 4, 2)
    y = lax.rem(col, 4)

    def step4(v, d):
        return lax.rem(v + d, 4)

    def at_x(d):
        return (row, step4(x, d) * 8 + zh * 4 + y)

    def at_y(d):
        return (row, x * 8 + zh * 4 + step4(y, d))

    def at_row(other):
        return (other, col)

    z_peer = (row, x * 8 + (1 - zh) * 4 + y)
    sibling = at_row(zl * 2 + 1 - core)

    barrier = pltpu.get_barrier_semaphore()
    peers = [at_x(d) for d in (1, 2, 3)] + [at_y(d) for d in (1, 2, 3)] + [z_peer]
    peers += [at_row(lax.rem(row + d, 8)) for d in range(1, 8)]
    for peer in peers:
        pl.semaphore_signal(barrier, inc=1, device_id=peer, device_id_type=MESH)

    def bring(n, src, dst):
        copy = pltpu.make_async_copy(src, dst, local_sem.at[n])
        copy.start()
        return copy

    pos_copy = bring(0, pos_hbm, pos_ref)
    cnt_copy = bring(8, cnt_hbm, cnt_ref)
    deg_copy = bring(1, deg_hbm, deg_ref)
    feat_copy = bring(2, feat_hbm, feat_ref)
    tiles_copy = bring(3, tiles_hbm, tiles)
    weight_copy = bring(4, weight_hbm, weight_v)
    cot_copy = bring(5, cot_hbm, cot_v)
    bias_copy = bring(6, bias_hbm, bias_ref)

    pos_copy.wait()
    cnt_copy.wait()
    pos = pos_ref[...]
    lane = lax.broadcasted_iota(I32, (1, slots), 1)
    live = lane < cnt_ref[...]
    lane2 = lax.broadcasted_iota(I32, (slots, slots), 1)
    sub2 = lax.broadcasted_iota(I32, (slots, slots), 0)
    eye = lane2 == sub2
    key_f = jnp.where(live, pos, 1024 + lane)
    key_b = jnp.where(live, (pos & 15) * 64 + (pos >> 4), 1024 + lane)
    order_f, sorted_f, same_f, last_f = segment_plan(key_f, 4, eye, lane2, sub2, slots)
    order_b, sorted_b, same_b, last_b = segment_plan(key_b, 6, eye, lane2, sub2, slots)
    rb = sorted_b & 63
    rb_x, rb_z, rb_y = rb >> 4, (rb >> 3) & 1, (rb >> 1) & 3
    slot_b = jnp.where((rb & 1) == 0, (rb_y * 4 + rb_x) * 2 + rb_z, 32 + (rb_x * 4 + rb_y) * 2 + rb_z)
    for n, line in enumerate((order_f, sorted_f & 15, same_f, last_f, order_b, slot_b, same_b, last_b)):
        table_v[pl.ds(n, 1), :] = line
    table_copy = bring(7, table_v, table)
    run[slots] = jnp.zeros((blk, run.shape[2]), BF16)

    deg_copy.wait()
    feat_copy.wait()
    eye_b = lax.broadcasted_iota(I32, (blk, blk), 0) == lax.broadcasted_iota(I32, (blk, blk), 1)
    scale_row = [lax.rsqrt(deg_ref[pl.ds(b, 1), :].astype(F32)) for b in range(2)]
    scale_col = [jnp.sum(jnp.where(eye_b, s, 0.0), axis=1, keepdims=True) for s in scale_row]
    for b in range(2):
        rows = pl.ds(b * blk, blk)
        gathered[row * 2 + b] = (scale_col[b] * feat_ref[rows, :].astype(F32)).astype(BF16)

    pl.semaphore_wait(barrier, len(peers))

    started = []

    def send(src, dst, device):
        n = len(started)
        copy = pltpu.make_async_remote_copy(
            src_ref=src, dst_ref=dst, send_sem=send_sem.at[n], recv_sem=recv_sem.at[n],
            device_id=device, device_id_type=MESH,
        )
        copy.start()
        started.append(copy)
        return copy

    def own_pair(r):
        return gathered.at[pl.ds(r * 2, 2)]

    far = [send(own_pair(row), own_pair(row), at_row(step4(zl, d) * 2 + core)) for d in (1, 2, 3)]
    near = [send(own_pair(row), own_pair(row), sibling)]

    for d in (1, 2, 3):
        far[d - 1].wait_recv()
        other = step4(zl, 4 - d) * 2 + core
        near.append(send(own_pair(other), own_pair(other), sibling))
    for copy in near:
        copy.wait_recv()

    table_copy.wait()
    tiles_copy.wait()

    def forward(g, acc):
        steps = [g * UNROLL + u for u in range(UNROLL)]
        terms = [dot(tiles[table[0, p] & (slots - 1)], gathered[table[1, p] & 15]) for p in steps]
        for p, term in zip(steps, terms):
            acc = acc * table[2, p].astype(F32) + term
            run[p] = acc.astype(BF16)
        return acc

    zero = jnp.zeros((blk, run.shape[2]), F32)
    lax.fori_loop(0, slots // UNROLL, forward, zero)

    def ending(line, segment):
        return jnp.clip(table[line, segment], 0, slots)

    def place(c, carry):
        cx, cz, cy = c // 8, lax.rem(c // 4, 2), lax.rem(c, 4)
        part[0, cy, cx, cz] = run[ending(3, c * 2)]
        part[1, cx, cy, cz] = run[ending(3, c * 2 + 1)]
        return carry

    lax.fori_loop(0, 32, place, 0)

    big, small = (y, x), (x, y)
    at_big, at_small = (at_y, at_x), (at_x, at_y)
    layers = (1 - zh, zh)
    both = (0, 1)
    copies = {}

    def issue(n, lay):
        for h in both:
            q = step4(small[h], OFFSETS[n])
            copies[h, lay, n] = [
                send(part.at[h, step4(big[h], d), q, layers[lay]], landed.at[h, lay, n, d - 1], at_big[h](d))
                for d in (2, 1, 3)
            ]

    def finish(n, lay):
        for h in both:
            q = step4(small[h], OFFSETS[n])
            total = part[h, big[h], q, layers[lay]].astype(F32)
            for d, c in zip((2, 1, 3), copies[h, lay, n]):
                c.wait_recv()
                total = total + landed[h, lay, n, d - 1].astype(F32)
            if n < 3:
                quarter[h, lay, n] = total.astype(BF16)
                copies[h, lay, "s", n] = send(
                    quarter.at[h, lay, n], landed_q.at[h, lay, n], at_small[h](OFFSETS[n])
                )
            else:
                own_small[h, lay] = total

    def small_finish(lay):
        for h in both:
            total = own_small[h, lay]
            for n in range(3):
                copies[h, lay, "s", n].wait_recv()
                total = total + landed_q[h, lay, n].astype(F32)
            if lay == 0:
                z_send[h] = total.astype(BF16)
                copies[h, "z"] = send(z_send.at[h], z_recv.at[h], z_peer)
            else:
                halves[h] = total

    for n in range(4):
        issue(n, 0)
    for n in range(4):
        finish(n, 0)
        issue(n, 1)
    small_finish(0)
    for n in range(4):
        finish(n, 1)
    small_finish(1)

    weight_copy.wait()
    cot_copy.wait()
    bias_copy.wait()
    weight = weight_v[...]
    bias = bias_ref[...]

    def spread(h, off, lay):
        ref = grads.at[h, big[h], step4(small[h], off), layers[lay]]
        copies[h, "b", off, lay] = [send(ref, ref, at_big[h](d)) for d in (2, 1, 3)]

    def spread_small(h, lay):
        ref = grads.at[h, big[h], small[h], layers[lay]]
        copies[h, "p", lay] = [send(ref, ref, at_small[h](d)) for d in (2, 1, 3)]

    def pass_on(lay):
        for d, n in ((1, 1), (3, 2), (2, 0)):
            for h in both:
                copies[h, "p", lay][n].wait_recv()
                spread(h, 4 - d, lay)

    for h in both:
        copies[h, "z"].wait_recv()
        hidden = scale_col[h] * (halves[h] + z_recv[h].astype(F32))
        upper, lower = two_parts(hidden)
        preact = dot(upper, weight) + dot(lower, weight) + bias
        gate = 1.0 / (1.0 + jnp.exp(-preact))
        rows = pl.ds(h * blk, blk)
        act_ref[rows, :] = (preact * gate).astype(BF16)
        grad_pre = cot_v[rows, :].astype(F32) * gate * (1.0 + preact * (1.0 - gate))
        hid_v[h] = hidden
        pre_v[h] = grad_pre
        upper, lower = two_parts(grad_pre)
        nt = ((1,), (1,))
        outgoing = scale_row[h] * (dot_general(weight, upper, nt) + dot_general(weight, lower, nt))
        grads[h, big[h], small[h], zh] = outgoing.astype(BF16)
        ref = grads.at[h, big[h], small[h], zh]
        copies[h, "g"] = send(ref, ref, z_peer)
        spread_small(h, 1)
        spread(h, 0, 1)

    out_copies = [bring(0, act_ref, act_hbm)]

    total = None
    bias_sum = None
    tn = ((0,), (0,))
    for h in both:
        hu, hl = two_parts(hid_v[h])
        gu, gl = two_parts(pre_v[h])
        term = dot_general(hu, gu, tn) + dot_general(hu, gl, tn) + dot_general(hl, gu, tn)
        sums = jnp.sum(pre_v[h], axis=0, keepdims=True)
        total = term if total is None else total + term
        bias_sum = sums if bias_sum is None else bias_sum + sums
    share = total.shape[0] // 8
    for r in range(8):
        gw_part[r % 2, r // 2, pl.ds(0, share), :] = total[r * share:(r + 1) * share, :]
        gw_part[r % 2, r // 2, pl.ds(share, 8), :] = jnp.broadcast_to(bias_sum, (8, bias_sum.shape[1]))
    gw_near = send(gw_part.at[1 - core], gw_in, sibling)

    pass_on(1)
    gw_near.wait_recv()
    for z in range(4):
        gw_sum[z] = gw_part[core, z] + gw_in[z]
    gw_row[zl] = gw_sum[zl]
    gw_far = []
    for d in (1, 2, 3):
        other = step4(zl, d)
        gw_far.append(send(gw_sum.at[other], gw_row.at[zl], at_row(other * 2 + core)))
    for h in both:
        copies[h, "g"].wait_recv()
        spread_small(h, 0)
        spread(h, 0, 0)
    pass_on(0)

    for copy in gw_far:
        copy.wait_recv()
    gw_z[zh] = gw_row[0] + gw_row[1] + gw_row[2] + gw_row[3]
    gw_across = send(gw_z.at[zh], gw_z.at[zh], z_peer)

    def arrive(lay):
        for off in (0, 1, 3, 2):
            for h in both:
                for copy in copies[h, "b", off, lay]:
                    copy.wait_recv()

    arrive(1)
    gw_across.wait_recv()
    gw_x[x] = gw_z[0] + gw_z[1]
    gw_along_x = [send(gw_x.at[x], gw_x.at[x], at_x(d)) for d in (1, 2, 3)]
    arrive(0)

    def backward(g, acc):
        steps = [g * UNROLL + u for u in range(UNROLL)]
        terms = [dot(flat_grad(table[5, p] & 63), tiles[table[4, p] & (slots - 1)]) for p in steps]
        for p, term in zip(steps, terms):
            acc = acc * table[6, p].astype(F32) + term
            run[p] = acc.astype(BF16)
        return acc

    def flat_grad(s):
        return grads[s // 32, lax.rem(s // 8, 4), lax.rem(s // 2, 4), lax.rem(s, 2)]

    zero_t = jnp.zeros((run.shape[1], blk), F32)
    lax.fori_loop(0, slots // UNROLL, backward, zero_t)

    def place_back(r, carry):
        for b in range(2):
            back[lax.rem(r, 2), r // 2, b] = run[ending(7, r * 2 + b)]
        return carry

    lax.fori_loop(0, 8, place_back, 0)

    near = []
    for d in (1, 2, 3, 0):
        other = step4(zl, d)
        near.append(send(back.at[1 - core, other], back_in.at[d], sibling))
    far = []
    for n, d in enumerate((1, 2, 3)):
        other = step4(zl, d)
        near[n].wait_recv()
        back_sum[n] = (back[core, other].astype(F32) + back_in[d].astype(F32)).astype(BF16)
        far.append(send(back_sum.at[n], back_recv.at[n], at_row(other * 2 + core)))
    for copy in gw_along_x:
        copy.wait_recv()
    gw_y[y] = gw_x[0] + gw_x[1] + gw_x[2] + gw_x[3]
    gw_along_y = [send(gw_y.at[y], gw_y.at[y], at_y(d)) for d in (1, 2, 3)]
    near[3].wait_recv()
    own = back[core, zl].astype(F32) + back_in[0].astype(F32)
    for copy in gw_along_y:
        copy.wait_recv()
    piece = gw_y[0] + gw_y[1] + gw_y[2] + gw_y[3]
    gb_ref[...] = piece[share:share + 1, :]
    gw_all[row] = piece[:share, :].astype(BF16)
    mine = gw_all.at[row]
    gw_out = [send(mine, mine, at_row(lax.rem(row + d, 8))) for d in range(1, 8)]
    for copy in gw_out:
        copy.wait_recv()
    for r in range(8):
        gw_ref[pl.ds(r * share, share), :] = gw_all[r].astype(F32)
    out_copies += [bring(1, gw_ref, gw_hbm), bring(2, gb_ref, gb_hbm)]
    for n in range(3):
        far[n].wait_recv()
        own = own + back_recv[n].astype(F32)
    for b in range(2):
        gf_ref[pl.ds(b * blk, blk), :] = jnp.transpose(scale_row[b] * own[b]).astype(BF16)

    out_copies.append(bring(3, gf_ref, gf_hbm))
    assert len(started) <= MAX_COPIES
    for copy in out_copies:
        copy.wait()
    for copy in started:
        copy.wait_send()


def deliver_kernel(*refs):
    ins, outs, held, sems = refs[:4], refs[4:8], refs[8:12], refs[12]
    moves = [pltpu.make_async_copy(ins[n], held[n], sems.at[n]) for n in range(4)]
    moves += [pltpu.make_async_copy(held[n], outs[n], sems.at[n + 4]) for n in range(4)]
    for move in moves[:4]:
        move.start()
    for n in range(4):
        moves[n].wait()
        moves[n + 4].start()
    for move in moves[4:]:
        move.wait()


def per_device(
    features, weight, bias_vector, cotangent, degrees, adjacency_tiles, tile_positions, tile_counts
):
    slots, blk = adjacency_tiles.shape[2:4]
    f_in, hid = weight.shape
    nodes = features.shape[0]
    share = f_in // 8
    anywhere = pl.BlockSpec(memory_space=pl.ANY)
    piece = (share + 8, hid)
    outs = pl.pallas_call(
        layer_kernel,
        out_shape=(
            jax.ShapeDtypeStruct((nodes, hid), BF16),
            jax.ShapeDtypeStruct((nodes, f_in), BF16),
            jax.ShapeDtypeStruct((f_in, hid), F32),
            jax.ShapeDtypeStruct((1, hid), F32),
        ),
        in_specs=[anywhere] * 8,
        out_specs=(anywhere,) * 4,
        scratch_shapes=[
            pltpu.VMEM((nodes, f_in), BF16),
            pltpu.VMEM((1, hid), F32),
            pltpu.VMEM((2, blk), I32),
            pltpu.VMEM((1, slots), I32),
            pltpu.VMEM((1, 1), I32),
            pltpu.VMEM((nodes, hid), BF16),
            pltpu.VMEM((nodes, f_in), BF16),
            pltpu.VMEM((f_in, hid), F32),
            pltpu.VMEM((1, hid), F32),
            pltpu.VMEM((slots, blk, blk), BF16),
            pltpu.VMEM((f_in, hid), BF16),
            pltpu.VMEM((nodes, hid), BF16),
            pltpu.VMEM((8, slots), I32),
            pltpu.SMEM((8, slots), I32),
            pltpu.VMEM((16, blk, f_in), BF16),
            pltpu.VMEM((slots + 1, blk, f_in), BF16),
            pltpu.VMEM((2, 4, 4, 2, blk, f_in), BF16),
            pltpu.VMEM((2, 2, 4, 3, blk, f_in), BF16),
            pltpu.VMEM((2, 2, 3, blk, f_in), BF16),
            pltpu.VMEM((2, 2, blk, f_in), F32),
            pltpu.VMEM((2, 2, 3, blk, f_in), BF16),
            pltpu.VMEM((2, blk, f_in), F32),
            pltpu.VMEM((2, blk, f_in), BF16),
            pltpu.VMEM((2, blk, f_in), BF16),
            pltpu.VMEM((2, 4, 4, 2, f_in, blk), BF16),
            pltpu.VMEM((2, blk, f_in), F32),
            pltpu.VMEM((2, blk, hid), F32),
            pltpu.VMEM((2, 4, 2, f_in, blk), BF16),
            pltpu.VMEM((4, 2, f_in, blk), BF16),
            pltpu.VMEM((3, 2, f_in, blk), BF16),
            pltpu.VMEM((3, 2, f_in, blk), BF16),
            pltpu.VMEM((2, 4) + piece, F32),
            pltpu.VMEM((4,) + piece, F32),
            pltpu.VMEM((4,) + piece, F32),
            pltpu.VMEM((4,) + piece, F32),
            pltpu.VMEM((4,) + piece, F32),
            pltpu.VMEM((4,) + piece, F32),
            pltpu.VMEM((2,) + piece, F32),
            pltpu.VMEM((8, share, hid), BF16),
            pltpu.SemaphoreType.DMA((9,)),
            pltpu.SemaphoreType.DMA((MAX_COPIES,)),
            pltpu.SemaphoreType.DMA((MAX_COPIES,)),
        ],
        compiler_params=pltpu.CompilerParams(
            collective_id=0, has_side_effects=True, vmem_limit_bytes=VMEM_BYTES
        ),
        name="graph_layer",
    )(
        features,
        weight,
        bias_vector.reshape(1, hid),
        cotangent,
        degrees.reshape(2, blk),
        adjacency_tiles.reshape(slots, blk, blk),
        tile_positions.reshape(1, slots),
        tile_counts,
    )
    activations, grad_features, grad_weight, grad_bias = pl.pallas_call(
        deliver_kernel,
        out_shape=tuple(jax.ShapeDtypeStruct(o.shape, o.dtype) for o in outs),
        in_specs=[anywhere] * 4,
        out_specs=(anywhere,) * 4,
        scratch_shapes=[pltpu.VMEM(o.shape, o.dtype) for o in outs] + [pltpu.SemaphoreType.DMA((8,))],
        compiler_params=pltpu.CompilerParams(vmem_limit_bytes=VMEM_BYTES),
        name="deliver",
    )(*outs)
    return activations, grad_features, grad_weight, grad_bias.reshape(hid)


def solution(mesh):
    placed = (
        P(("row", "col"), None),
        P(),
        P(),
        P(("row", "col"), None),
        P(("row", "col")),
        P("row", "col", None, None, None),
        P("row", "col", None),
        P("row", "col"),
    )
    return jax.shard_map(
        per_device,
        mesh=mesh,
        in_specs=placed,
        out_specs=(P(("row", "col"), None), P(("row", "col"), None), P(), P()),
        check_vma=False,
    )
```

time: 93.2 us -> 77 us (0.83); the launches traced: 91.7 us -> 76.9 us
  local copies, waits for them, and re-layouts: 9.28 us -> 0 us
  Pallas kernels: 81.2 us -> 75.6 us
    unnamed x18 -> x0, local copies, waits for them, and re-layouts: 9.28 us -> none
    pallas_call x1, Pallas kernels: 81.2 us -> 73.9 us  [per_device(): pl.pallas_call(layer_kernel, out_shape=(jax.ShapeDtypeStruct((nodes, hid)...]
    pallas_call x0 -> x1, Pallas kernels: none -> 1.73 us  [per_device(): pl.pallas_call(deliver_kernel, out_shape=tuple((jax.ShapeDtypeStruct(o.sh...]
where the time goes in v2:
time: 77 us; the launch traced here: 76.9 us
  Pallas kernels  75.6 us (98%)
  between operations  1.29 us (2%)
    pallas_call x1, Pallas kernels, per_device(): pl.pallas_call(layer_kernel, out_shape=(jax.ShapeDtypeStruct((nodes, hid)...  73.9 us
    pallas_call x1, Pallas kernels, per_device(): pl.pallas_call(deliver_kernel, out_shape=tuple((jax.ShapeDtypeStruct(o.sh...  1.73 us

profile of v2, /device:TPU:1, one launch (start us, length us, event | category | flops | bytes accessed | tf_op | source)
XLA Modules:
  0.0 76.9 jit_solution(6792244260737535417)
XLA Ops:
  1.3 73.9 %graph_layer.1 = (bf16[256,256]{1,0:T(8,128)(2,1)}, bf16[256,128]{1,0:T(8,128)(2,1)}, f32[128,256]{1,0:T(8,128)}, f32[1,256]{1,0:T(1,128)}) custom-call(bf16[256,128]{1,0:T(8,128)(2,1)} %feat_hbm.1, bf16[128,256]{1,0:T(8,128)(2,1)} %weight_hbm.1, f32[1,256]{1,0:T(1,128)} %bitcast.6, bf16[256,256]{1,0:T(8,128)(2,1)} %cot_hbm.1, s32[2,128]{1,0:T(2,128)} %bitcast.7, ...), custom_call_target="tpu_custom_call" | custom-call | tf_op jit(solution)/shard_map/graph_layer/pallas_call | solution.py:411
  75.2 1.7 %deliver.1 = (bf16[256,256]{1,0:T(8,128)(2,1)}, bf16[256,128]{1,0:T(8,128)(2,1)}, f32[128,256]{1,0:T(8,128)}, f32[1,256]{1,0:T(1,128)}) custom-call(bf16[256,256]{1,0:T(8,128)(2,1)} %get-tuple-element.12.refs_0_, bf16[256,128]{1,0:T(8,128)(2,1)} %get-tuple-element.13.refs_1_, f32[128,256]{1,0:T(8,128)} %get-tuple-element.14.refs_2_, ...), custom_call_target="tpu_custom_call" | custom-call | tf_op jit(solution)/shard_map/deliver/pallas_call | solution.py:479

commit v3 on v2

--- a/solution.py
+++ b/solution.py
@@ -10,9 +10,10 @@
 BF16 = jnp.bfloat16
 I32 = jnp.int32
 UNROLL = 32
-MAX_COPIES = 192
+ARRIVALS = 53
+LOTS = 11
 OFFSETS = (2, 1, 3, 0)
-VMEM_BYTES = 60 * 1024 * 1024
+VMEM_BYTES = 40 * 1024 * 1024
 
 
 def two_parts(values):
@@ -51,11 +52,11 @@
 
 def layer_kernel(
     feat_hbm, weight_hbm, bias_hbm, cot_hbm, deg_hbm, tiles_hbm, pos_hbm, cnt_hbm,
-    act_hbm, gf_hbm, gw_hbm, gb_hbm,
-    feat_ref, bias_ref, deg_ref, pos_ref, cnt_ref, act_ref, gf_ref, gw_ref, gb_ref,
+    act_ref, gf_ref, gw_ref, gb_ref,
+    feat_ref, bias_ref, deg_ref, pos_ref, cnt_ref,
     tiles, weight_v, cot_v, table_v, table, gathered, run, part, landed, quarter, own_small,
     landed_q, halves, z_send, z_recv, grads, hid_v, pre_v, back, back_in, back_sum, back_recv,
-    gw_part, gw_in, gw_sum, gw_row, gw_x, gw_y, gw_z, gw_all, local_sem, send_sem, recv_sem,
+    gw_part, gw_in, gw_sum, gw_row, gw_x, gw_y, gw_z, gw_all, gw_wait, local_sem, send_sem, recv_sem,
 ):
     slots, blk, _ = tiles.shape
     row = lax.axis_index("row")
@@ -132,30 +133,35 @@
 
     pl.semaphore_wait(barrier, len(peers))
 
-    started = []
-
-    def send(src, dst, device):
-        n = len(started)
+    slot_of, lots = {}, {}
+
+    def arrival(key):
+        return recv_sem.at[slot_of.setdefault(key, len(slot_of))]
+
+    def send(src, dst, device, key, lot):
         copy = pltpu.make_async_remote_copy(
-            src_ref=src, dst_ref=dst, send_sem=send_sem.at[n], recv_sem=recv_sem.at[n],
+            src_ref=src, dst_ref=dst, send_sem=send_sem.at[lot], recv_sem=arrival(key),
             device_id=device, device_id_type=MESH,
         )
         copy.start()
-        started.append(copy)
+        lots[lot] = lots.get(lot, 0) + 1
         return copy
+
+    def wait_all(ref, sem):
+        pltpu.make_async_copy(ref, ref, sem).wait()
 
     def own_pair(r):
         return gathered.at[pl.ds(r * 2, 2)]
 
-    far = [send(own_pair(row), own_pair(row), at_row(step4(zl, d) * 2 + core)) for d in (1, 2, 3)]
-    near = [send(own_pair(row), own_pair(row), sibling)]
+    mine = own_pair(row)
+    far = [send(mine, mine, at_row(step4(zl, d) * 2 + core), ("feat", d), 0) for d in (1, 2, 3)]
+    send(mine, mine, sibling, "feat", 0)
 
     for d in (1, 2, 3):
         far[d - 1].wait_recv()
         other = step4(zl, 4 - d) * 2 + core
-        near.append(send(own_pair(other), own_pair(other), sibling))
-    for copy in near:
-        copy.wait_recv()
+        send(own_pair(other), own_pair(other), sibling, "feat", 0)
+    wait_all(gathered.at[pl.ds(0, 8)], arrival("feat"))
 
     table_copy.wait()
     tiles_copy.wait()
@@ -191,35 +197,33 @@
     def issue(n, lay):
         for h in both:
             q = step4(small[h], OFFSETS[n])
-            copies[h, lay, n] = [
-                send(part.at[h, step4(big[h], d), q, layers[lay]], landed.at[h, lay, n, d - 1], at_big[h](d))
-                for d in (2, 1, 3)
-            ]
+            for d in (2, 1, 3):
+                src = part.at[h, step4(big[h], d), q, layers[lay]]
+                send(src, landed.at[h, lay, n, d - 1], at_big[h](d), ("big", h, lay, n), 1 + lay)
 
     def finish(n, lay):
         for h in both:
             q = step4(small[h], OFFSETS[n])
+            wait_all(landed.at[h, lay, n], arrival(("big", h, lay, n)))
             total = part[h, big[h], q, layers[lay]].astype(F32)
-            for d, c in zip((2, 1, 3), copies[h, lay, n]):
-                c.wait_recv()
+            for d in (2, 1, 3):
                 total = total + landed[h, lay, n, d - 1].astype(F32)
             if n < 3:
                 quarter[h, lay, n] = total.astype(BF16)
-                copies[h, lay, "s", n] = send(
-                    quarter.at[h, lay, n], landed_q.at[h, lay, n], at_small[h](OFFSETS[n])
-                )
+                src, dst = quarter.at[h, lay, n], landed_q.at[h, lay, n]
+                send(src, dst, at_small[h](OFFSETS[n]), ("small", h, lay), 3)
             else:
                 own_small[h, lay] = total
 
     def small_finish(lay):
         for h in both:
+            wait_all(landed_q.at[h, lay], arrival(("small", h, lay)))
             total = own_small[h, lay]
             for n in range(3):
-                copies[h, lay, "s", n].wait_recv()
                 total = total + landed_q[h, lay, n].astype(F32)
             if lay == 0:
                 z_send[h] = total.astype(BF16)
-                copies[h, "z"] = send(z_send.at[h], z_recv.at[h], z_peer)
+                copies[h, "z"] = send(z_send.at[h], z_recv.at[h], z_peer, ("z", h), 3)
             else:
                 halves[h] = total
 
@@ -241,16 +245,18 @@
 
     def spread(h, off, lay):
         ref = grads.at[h, big[h], step4(small[h], off), layers[lay]]
-        copies[h, "b", off, lay] = [send(ref, ref, at_big[h](d)) for d in (2, 1, 3)]
+        for d in (2, 1, 3):
+            send(ref, ref, at_big[h](d), ("spread", lay), 4 + lay)
 
     def spread_small(h, lay):
         ref = grads.at[h, big[h], small[h], layers[lay]]
-        copies[h, "p", lay] = [send(ref, ref, at_small[h](d)) for d in (2, 1, 3)]
+        for d in (2, 1, 3):
+            copies[h, "p", lay, d] = send(ref, ref, at_small[h](d), ("pass", h, lay, d), 6)
 
     def pass_on(lay):
-        for d, n in ((1, 1), (3, 2), (2, 0)):
+        for d in (1, 3, 2):
             for h in both:
-                copies[h, "p", lay][n].wait_recv()
+                copies[h, "p", lay, d].wait_recv()
                 spread(h, 4 - d, lay)
 
     for h in both:
@@ -269,11 +275,9 @@
         outgoing = scale_row[h] * (dot_general(weight, upper, nt) + dot_general(weight, lower, nt))
         grads[h, big[h], small[h], zh] = outgoing.astype(BF16)
         ref = grads.at[h, big[h], small[h], zh]
-        copies[h, "g"] = send(ref, ref, z_peer)
+        copies[h, "g"] = send(ref, ref, z_peer, ("g", h), 3)
         spread_small(h, 1)
         spread(h, 0, 1)
-
-    out_copies = [bring(0, act_ref, act_hbm)]
 
     total = None
     bias_sum = None
@@ -289,38 +293,38 @@
     for r in range(8):
         gw_part[r % 2, r // 2, pl.ds(0, share), :] = total[r * share:(r + 1) * share, :]
         gw_part[r % 2, r // 2, pl.ds(share, 8), :] = jnp.broadcast_to(bias_sum, (8, bias_sum.shape[1]))
-    gw_near = send(gw_part.at[1 - core], gw_in, sibling)
-
-    pass_on(1)
+    gw_near = send(gw_part.at[1 - core], gw_in, sibling, "gw near", 7)
+
     gw_near.wait_recv()
     for z in range(4):
         gw_sum[z] = gw_part[core, z] + gw_in[z]
     gw_row[zl] = gw_sum[zl]
-    gw_far = []
     for d in (1, 2, 3):
         other = step4(zl, d)
-        gw_far.append(send(gw_sum.at[other], gw_row.at[zl], at_row(other * 2 + core)))
+        send(gw_sum.at[other], gw_row.at[zl], at_row(other * 2 + core), "gw far", 8)
+    pass_on(1)
     for h in both:
         copies[h, "g"].wait_recv()
         spread_small(h, 0)
         spread(h, 0, 0)
+    wait_all(gw_row.at[pl.ds(0, 3)], arrival("gw far"))
+    gw_z[zh] = gw_row[0] + gw_row[1] + gw_row[2] + gw_row[3]
+    gw_across = send(gw_z.at[zh], gw_z.at[zh], z_peer, "gw z", 8)
+
     pass_on(0)
 
-    for copy in gw_far:
-        copy.wait_recv()
-    gw_z[zh] = gw_row[0] + gw_row[1] + gw_row[2] + gw_row[3]
-    gw_across = send(gw_z.at[zh], gw_z.at[zh], z_peer)
-
     def arrive(lay):
-        for off in (0, 1, 3, 2):
-            for h in both:
-                for copy in copies[h, "b", off, lay]:
-                    copy.wait_recv()
-
-    arrive(1)
+        wait_all(tiles.at[pl.ds(0, 24)], arrival(("spread", lay)))
+
     gw_across.wait_recv()
     gw_x[x] = gw_z[0] + gw_z[1]
-    gw_along_x = [send(gw_x.at[x], gw_x.at[x], at_x(d)) for d in (1, 2, 3)]
+    for d in (1, 2, 3):
+        send(gw_x.at[x], gw_x.at[x], at_x(d), "gw x", 8)
+    arrive(1)
+    wait_all(gw_x.at[pl.ds(0, 3)], arrival("gw x"))
+    gw_y[y] = gw_x[0] + gw_x[1] + gw_x[2] + gw_x[3]
+    for d in (1, 2, 3):
+        send(gw_y.at[y], gw_y.at[y], at_y(d), "gw y", 8)
     arrive(0)
 
     def backward(g, acc):
@@ -336,6 +340,13 @@
 
     zero_t = jnp.zeros((run.shape[1], blk), F32)
     lax.fori_loop(0, slots // UNROLL, backward, zero_t)
+    wait_all(gw_y.at[pl.ds(0, 3)], arrival("gw y"))
+    piece = gw_y[0] + gw_y[1] + gw_y[2] + gw_y[3]
+    gb_ref[...] = piece[share:share + 1, :]
+    gw_all[row] = piece[:share, :].astype(BF16)
+    mine = gw_all.at[row]
+    for d in range(1, 8):
+        send(mine, mine, at_row(lax.rem(row + d, 8)), "gw out", 10)
 
     def place_back(r, carry):
         for b in range(2):
@@ -347,55 +358,43 @@
     near = []
     for d in (1, 2, 3, 0):
         other = step4(zl, d)
-        near.append(send(back.at[1 - core, other], back_in.at[d], sibling))
-    far = []
+        near.append(send(back.at[1 - core, other], back_in.at[d], sibling, ("back", d), 9))
     for n, d in enumerate((1, 2, 3)):
         other = step4(zl, d)
         near[n].wait_recv()
         back_sum[n] = (back[core, other].astype(F32) + back_in[d].astype(F32)).astype(BF16)
-        far.append(send(back_sum.at[n], back_recv.at[n], at_row(other * 2 + core)))
-    for copy in gw_along_x:
-        copy.wait_recv()
-    gw_y[y] = gw_x[0] + gw_x[1] + gw_x[2] + gw_x[3]
-    gw_along_y = [send(gw_y.at[y], gw_y.at[y], at_y(d)) for d in (1, 2, 3)]
+        send(back_sum.at[n], back_recv.at[n], at_row(other * 2 + core), "back", 9)
     near[3].wait_recv()
     own = back[core, zl].astype(F32) + back_in[0].astype(F32)
-    for copy in gw_along_y:
-        copy.wait_recv()
-    piece = gw_y[0] + gw_y[1] + gw_y[2] + gw_y[3]
-    gb_ref[...] = piece[share:share + 1, :]
-    gw_all[row] = piece[:share, :].astype(BF16)
-    mine = gw_all.at[row]
-    gw_out = [send(mine, mine, at_row(lax.rem(row + d, 8))) for d in range(1, 8)]
-    for copy in gw_out:
-        copy.wait_recv()
+    wait_all(gw_all.at[pl.ds(0, 7)], arrival("gw out"))
     for r in range(8):
         gw_ref[pl.ds(r * share, share), :] = gw_all[r].astype(F32)
-    out_copies += [bring(1, gw_ref, gw_hbm), bring(2, gb_ref, gb_hbm)]
+    wait_all(back_recv, arrival("back"))
     for n in range(3):
-        far[n].wait_recv()
         own = own + back_recv[n].astype(F32)
     for b in range(2):
         gf_ref[pl.ds(b * blk, blk), :] = jnp.transpose(scale_row[b] * own[b]).astype(BF16)
 
-    out_copies.append(bring(3, gf_ref, gf_hbm))
-    assert len(started) <= MAX_COPIES
-    for copy in out_copies:
-        copy.wait()
-    for copy in started:
-        copy.wait_send()
+    assert len(slot_of) == ARRIVALS
+    pairs = {0, 9}
+    for lot, count in lots.items():
+        if lot == 7:
+            ref = gw_in
+        elif lot == 8:
+            ref = gw_wait.at[pl.ds(0, count)]
+        elif lot == 10:
+            ref = gw_all.at[pl.ds(0, count)]
+        else:
+            ref = tiles.at[pl.ds(0, count * 2 if lot in pairs else count)]
+        wait_all(ref, send_sem.at[lot])
 
 
 def deliver_kernel(*refs):
-    ins, outs, held, sems = refs[:4], refs[4:8], refs[8:12], refs[12]
-    moves = [pltpu.make_async_copy(ins[n], held[n], sems.at[n]) for n in range(4)]
-    moves += [pltpu.make_async_copy(held[n], outs[n], sems.at[n + 4]) for n in range(4)]
-    for move in moves[:4]:
+    sems = refs[8]
+    moves = [pltpu.make_async_copy(refs[n], refs[n + 4], sems.at[n]) for n in range(4)]
+    for move in moves:
         move.start()
-    for n in range(4):
-        moves[n].wait()
-        moves[n + 4].start()
-    for move in moves[4:]:
+    for move in moves:
         move.wait()
 
 
@@ -408,26 +407,27 @@
     share = f_in // 8
     anywhere = pl.BlockSpec(memory_space=pl.ANY)
     piece = (share + 8, hid)
+    vmem = pl.BlockSpec(memory_space=pltpu.VMEM)
+
+    def in_hbm(value):
+        return pltpu.with_memory_space_constraint(value, pltpu.HBM)
+
     outs = pl.pallas_call(
         layer_kernel,
         out_shape=(
-            jax.ShapeDtypeStruct((nodes, hid), BF16),
-            jax.ShapeDtypeStruct((nodes, f_in), BF16),
-            jax.ShapeDtypeStruct((f_in, hid), F32),
-            jax.ShapeDtypeStruct((1, hid), F32),
+            pltpu.VMEM((nodes, hid), BF16),
+            pltpu.VMEM((nodes, f_in), BF16),
+            pltpu.VMEM((f_in, hid), F32),
+            pltpu.VMEM((1, hid), F32),
         ),
         in_specs=[anywhere] * 8,
-        out_specs=(anywhere,) * 4,
+        out_specs=(vmem,) * 4,
         scratch_shapes=[
             pltpu.VMEM((nodes, f_in), BF16),
             pltpu.VMEM((1, hid), F32),
             pltpu.VMEM((2, blk), I32),
             pltpu.VMEM((1, slots), I32),
             pltpu.VMEM((1, 1), I32),
-            pltpu.VMEM((nodes, hid), BF16),
-            pltpu.VMEM((nodes, f_in), BF16),
-            pltpu.VMEM((f_in, hid), F32),
-            pltpu.VMEM((1, hid), F32),
             pltpu.VMEM((slots, blk, blk), BF16),
             pltpu.VMEM((f_in, hid), BF16),
             pltpu.VMEM((nodes, hid), BF16),
@@ -458,33 +458,33 @@
             pltpu.VMEM((4,) + piece, F32),
             pltpu.VMEM((2,) + piece, F32),
             pltpu.VMEM((8, share, hid), BF16),
+            pltpu.VMEM((10,) + piece, F32),
             pltpu.SemaphoreType.DMA((9,)),
-            pltpu.SemaphoreType.DMA((MAX_COPIES,)),
-            pltpu.SemaphoreType.DMA((MAX_COPIES,)),
+            pltpu.SemaphoreType.DMA((LOTS,)),
+            pltpu.SemaphoreType.DMA((ARRIVALS,)),
         ],
         compiler_params=pltpu.CompilerParams(
             collective_id=0, has_side_effects=True, vmem_limit_bytes=VMEM_BYTES
         ),
         name="graph_layer",
     )(
-        features,
-        weight,
-        bias_vector.reshape(1, hid),
-        cotangent,
-        degrees.reshape(2, blk),
-        adjacency_tiles.reshape(slots, blk, blk),
-        tile_positions.reshape(1, slots),
+        in_hbm(features),
+        in_hbm(weight),
+        in_hbm(bias_vector.reshape(1, hid)),
+        in_hbm(cotangent),
+        in_hbm(degrees.reshape(2, blk)),
+        in_hbm(adjacency_tiles.reshape(slots, blk, blk)),
+        in_hbm(tile_positions.reshape(1, slots)),
         tile_counts,
     )
     activations, grad_features, grad_weight, grad_bias = pl.pallas_call(
         deliver_kernel,
-        out_shape=tuple(jax.ShapeDtypeStruct(o.shape, o.dtype) for o in outs),
-        in_specs=[anywhere] * 4,
-        out_specs=(anywhere,) * 4,
-        scratch_shapes=[pltpu.VMEM(o.shape, o.dtype) for o in outs] + [pltpu.SemaphoreType.DMA((8,))],
-        compiler_params=pltpu.CompilerParams(vmem_limit_bytes=VMEM_BYTES),
+        out_shape=tuple(pltpu.HBM(o.shape, o.dtype) for o in outs),
+        in_specs=[vmem] * 4,
+        out_specs=(pl.BlockSpec(memory_space=pltpu.HBM),) * 4,
+        scratch_shapes=[pltpu.SemaphoreType.DMA((4,))],
         name="deliver",
-    )(*outs)
+    )(*(pltpu.with_memory_space_constraint(o, pltpu.VMEM) for o in outs))
     return activations, grad_features, grad_weight, grad_bias.reshape(hid)
 
 

time: 77 us -> 72.1 us (0.936)
  Pallas kernels: 75.6 us -> 70.7 us
    pallas_call x2, Pallas kernels: 75.6 us -> 70.7 us  [the longest x1 70 us: per_device(): pl.pallas_call(layer_kernel, out_shape=(pltpu.VMEM((nodes, hid), BF16), p...]
where the time goes in v3:
time: 72.1 us; the launch traced here: 72 us
  Pallas kernels  70.7 us (98%)
  between operations  1.29 us (2%)
    pallas_call x1, Pallas kernels, per_device(): pl.pallas_call(layer_kernel, out_shape=(pltpu.VMEM((nodes, hid), BF16), p...  70 us

profile of v3, /device:TPU:1, one launch (start us, length us, event | category | flops | bytes accessed | tf_op | source)
XLA Modules:
  0.0 72.0 jit_solution(11149338999897559073)
XLA Ops:
  1.3 70.0 %graph_layer.1 = (bf16[256,256]{1,0:T(8,128)(2,1)S(1)}, bf16[256,128]{1,0:T(8,128)(2,1)S(1)}, f32[128,256]{1,0:T(8,128)S(1)}, f32[1,256]{1,0:T(1,128)S(1)}) custom-call(bf16[256,128]{1,0:T(8,128)(2,1)} %feat_hbm.1, bf16[128,256]{1,0:T(8,128)(2,1)} %weight_hbm.1, f32[1,256]{1,0:T(1,128)} %bitcast.6, bf16[256,256]{1,0:T(8,128)(2,1)} %cot_hbm.1, ...), custom_call_target="tpu_custom_call" | custom-call | tf_op jit(solution)/shard_map/graph_layer/pallas_call | solution.py:415
  71.3 0.8 %deliver.1 = (bf16[256,256]{1,0:T(8,128)(2,1)}, bf16[256,128]{1,0:T(8,128)(2,1)}, f32[128,256]{1,0:T(8,128)}, f32[1,256]{1,0:T(1,128)}) custom-call(bf16[256,256]{1,0:T(8,128)(2,1)S(1)} %get-tuple-element.12.refs_0_, bf16[256,128]{1,0:T(8,128)(2,1)S(1)} %get-tuple-element.13.refs_1_, f32[128,256]{1,0:T(8,128)S(1)} %get-tuple-element.14.refs_2_, ...), custom_call_target="tpu_custom_call" | custom-call | tf_op jit(solution)/shard_map/deliver/pallas_call | solution.py:480

commit v4 on v3

--- a/solution.py
+++ b/solution.py
@@ -10,9 +10,10 @@
 BF16 = jnp.bfloat16
 I32 = jnp.int32
 UNROLL = 32
-ARRIVALS = 53
+ARRIVALS = 61
 LOTS = 11
 OFFSETS = (2, 1, 3, 0)
+RELAYED = {(0, 1): 1, (3, 1): 3, (1, 1): 1, (2, 1): 3, (0, 0): 1}
 VMEM_BYTES = 40 * 1024 * 1024
 
 
@@ -56,7 +57,7 @@
     feat_ref, bias_ref, deg_ref, pos_ref, cnt_ref,
     tiles, weight_v, cot_v, table_v, table, gathered, run, part, landed, quarter, own_small,
     landed_q, halves, z_send, z_recv, grads, hid_v, pre_v, back, back_in, back_sum, back_recv,
-    gw_part, gw_in, gw_sum, gw_row, gw_x, gw_y, gw_z, gw_all, gw_wait, local_sem, send_sem, recv_sem,
+    gw_part, gw_in, gw_sum, gw_row, gw_x, gw_y, gw_z, gw_all, gw_wait, local_sem, send_sem, recv_sem, feat_sem,
 ):
     slots, blk, _ = tiles.shape
     row = lax.axis_index("row")
@@ -79,12 +80,14 @@
     def at_row(other):
         return (other, col)
 
+    half = zl // 2
+    chips = (3 - 3 * half, 2 - half, zl + 1 - 2 * lax.rem(zl, 2))
     z_peer = (row, x * 8 + (1 - zh) * 4 + y)
     sibling = at_row(zl * 2 + 1 - core)
 
     barrier = pltpu.get_barrier_semaphore()
     peers = [at_x(d) for d in (1, 2, 3)] + [at_y(d) for d in (1, 2, 3)] + [z_peer]
-    peers += [at_row(lax.rem(row + d, 8)) for d in range(1, 8)]
+    peers += [at_row(other * 2 + core) for other in chips] + [sibling]
     for peer in peers:
         pl.semaphore_signal(barrier, inc=1, device_id=peer, device_id_type=MESH)
 
@@ -135,12 +138,14 @@
 
     slot_of, lots = {}, {}
 
-    def arrival(key):
+    def arrival(key, chip=None):
+        if chip is not None:
+            return feat_sem.at[chip]
         return recv_sem.at[slot_of.setdefault(key, len(slot_of))]
 
-    def send(src, dst, device, key, lot):
+    def send(src, dst, device, key, lot, chip=None):
         copy = pltpu.make_async_remote_copy(
-            src_ref=src, dst_ref=dst, send_sem=send_sem.at[lot], recv_sem=arrival(key),
+            src_ref=src, dst_ref=dst, send_sem=send_sem.at[lot], recv_sem=arrival(key, chip),
             device_id=device, device_id_type=MESH,
         )
         copy.start()
@@ -154,12 +159,13 @@
         return gathered.at[pl.ds(r * 2, 2)]
 
     mine = own_pair(row)
-    far = [send(mine, mine, at_row(step4(zl, d) * 2 + core), ("feat", d), 0) for d in (1, 2, 3)]
+    for other in chips:
+        send(mine, mine, at_row(other * 2 + core), "feat far", 0, zl)
     send(mine, mine, sibling, "feat", 0)
 
-    for d in (1, 2, 3):
-        far[d - 1].wait_recv()
-        other = step4(zl, 4 - d) * 2 + core
+    for chip in (chips[2], chips[1], chips[0]):
+        wait_all(mine, arrival("feat far", chip))
+        other = chip * 2 + core
         send(own_pair(other), own_pair(other), sibling, "feat", 0)
     wait_all(gathered.at[pl.ds(0, 8)], arrival("feat"))
 
@@ -245,8 +251,17 @@
 
     def spread(h, off, lay):
         ref = grads.at[h, big[h], step4(small[h], off), layers[lay]]
-        for d in (2, 1, 3):
-            send(ref, ref, at_big[h](d), ("spread", lay), 4 + lay)
+        way = RELAYED.get((off, lay))
+        for d in (1, 3) if way else (2, 1, 3):
+            key = ("relay", h, off, lay) if d == way else ("spread", lay)
+            copies[h, off, lay, d] = send(ref, ref, at_big[h](d), key, 4 + lay)
+
+    def relay(off, lay):
+        way = RELAYED[off, lay]
+        for h in both:
+            copies[h, off, lay, way].wait_recv()
+            ref = grads.at[h, step4(big[h], 4 - way), step4(small[h], off), layers[lay]]
+            send(ref, ref, at_big[h](way), ("spread", lay), 4 + lay)
 
     def spread_small(h, lay):
         ref = grads.at[h, big[h], small[h], layers[lay]]
@@ -303,28 +318,30 @@
         other = step4(zl, d)
         send(gw_sum.at[other], gw_row.at[zl], at_row(other * 2 + core), "gw far", 8)
     pass_on(1)
+    relay(0, 1)
     for h in both:
         copies[h, "g"].wait_recv()
         spread_small(h, 0)
         spread(h, 0, 0)
+    relay(3, 1)
+    relay(1, 1)
+    relay(2, 1)
     wait_all(gw_row.at[pl.ds(0, 3)], arrival("gw far"))
     gw_z[zh] = gw_row[0] + gw_row[1] + gw_row[2] + gw_row[3]
     gw_across = send(gw_z.at[zh], gw_z.at[zh], z_peer, "gw z", 8)
 
     pass_on(0)
+    relay(0, 0)
 
     def arrive(lay):
-        wait_all(tiles.at[pl.ds(0, 24)], arrival(("spread", lay)))
+        relayed = sum(1 for _, other in RELAYED if other == lay)
+        wait_all(tiles.at[pl.ds(0, 24 - 2 * relayed)], arrival(("spread", lay)))
 
     gw_across.wait_recv()
     gw_x[x] = gw_z[0] + gw_z[1]
     for d in (1, 2, 3):
         send(gw_x.at[x], gw_x.at[x], at_x(d), "gw x", 8)
     arrive(1)
-    wait_all(gw_x.at[pl.ds(0, 3)], arrival("gw x"))
-    gw_y[y] = gw_x[0] + gw_x[1] + gw_x[2] + gw_x[3]
-    for d in (1, 2, 3):
-        send(gw_y.at[y], gw_y.at[y], at_y(d), "gw y", 8)
     arrive(0)
 
     def backward(g, acc):
@@ -339,39 +356,48 @@
         return grads[s // 32, lax.rem(s // 8, 4), lax.rem(s // 2, 4), lax.rem(s, 2)]
 
     zero_t = jnp.zeros((run.shape[1], blk), F32)
-    lax.fori_loop(0, slots // UNROLL, backward, zero_t)
+    middle = slots // UNROLL // 2
+    acc = lax.fori_loop(0, middle, backward, zero_t)
+    wait_all(gw_x.at[pl.ds(0, 3)], arrival("gw x"))
+    gw_y[y] = gw_x[0] + gw_x[1] + gw_x[2] + gw_x[3]
+    for d in (1, 2, 3):
+        send(gw_y.at[y], gw_y.at[y], at_y(d), "gw y", 8)
+    lax.fori_loop(middle, slots // UNROLL, backward, acc)
+    def place_back(r, carry):
+        for b in range(2):
+            back[lax.rem(r, 2), r // 2, b] = run[ending(7, r * 2 + b)]
+        return carry
+
+    lax.fori_loop(0, 8, place_back, 0)
+
+    near = []
+    for n, other in enumerate((*chips, zl)):
+        near.append(send(back.at[1 - core, other], back_in.at[n], sibling, ("back", n), 9))
     wait_all(gw_y.at[pl.ds(0, 3)], arrival("gw y"))
     piece = gw_y[0] + gw_y[1] + gw_y[2] + gw_y[3]
     gb_ref[...] = piece[share:share + 1, :]
     gw_all[row] = piece[:share, :].astype(BF16)
     mine = gw_all.at[row]
-    for d in range(1, 8):
-        send(mine, mine, at_row(lax.rem(row + d, 8)), "gw out", 10)
-
-    def place_back(r, carry):
-        for b in range(2):
-            back[lax.rem(r, 2), r // 2, b] = run[ending(7, r * 2 + b)]
-        return carry
-
-    lax.fori_loop(0, 8, place_back, 0)
-
-    near = []
-    for d in (1, 2, 3, 0):
-        other = step4(zl, d)
-        near.append(send(back.at[1 - core, other], back_in.at[d], sibling, ("back", d), 9))
-    for n, d in enumerate((1, 2, 3)):
-        other = step4(zl, d)
+    for other in chips:
+        send(mine, mine, at_row(other * 2 + core), "gw out", 10)
+    send(mine, mine, sibling, "gw pass", 10)
+
+    for n, other in enumerate(chips):
         near[n].wait_recv()
-        back_sum[n] = (back[core, other].astype(F32) + back_in[d].astype(F32)).astype(BF16)
-        send(back_sum.at[n], back_recv.at[n], at_row(other * 2 + core), "back", 9)
+        back_sum[n] = (back[core, other].astype(F32) + back_in[n].astype(F32)).astype(BF16)
+        send(back_sum.at[n], back_recv.at[zl], at_row(other * 2 + core), "back", 9)
     near[3].wait_recv()
-    own = back[core, zl].astype(F32) + back_in[0].astype(F32)
-    wait_all(gw_all.at[pl.ds(0, 7)], arrival("gw out"))
+    own = back[core, zl].astype(F32) + back_in[3].astype(F32)
+    wait_all(gw_all.at[pl.ds(0, 3)], arrival("gw out"))
+    for chip in chips:
+        passed = gw_all.at[chip * 2 + core]
+        send(passed, passed, sibling, "gw pass", 10)
+    wait_all(gw_all.at[pl.ds(0, 4)], arrival("gw pass"))
     for r in range(8):
         gw_ref[pl.ds(r * share, share), :] = gw_all[r].astype(F32)
-    wait_all(back_recv, arrival("back"))
-    for n in range(3):
-        own = own + back_recv[n].astype(F32)
+    wait_all(back_recv.at[pl.ds(0, 3)], arrival("back"))
+    for other in chips:
+        own = own + back_recv[other].astype(F32)
     for b in range(2):
         gf_ref[pl.ds(b * blk, blk), :] = jnp.transpose(scale_row[b] * own[b]).astype(BF16)
 
@@ -449,7 +475,7 @@
             pltpu.VMEM((2, 4, 2, f_in, blk), BF16),
             pltpu.VMEM((4, 2, f_in, blk), BF16),
             pltpu.VMEM((3, 2, f_in, blk), BF16),
-            pltpu.VMEM((3, 2, f_in, blk), BF16),
+            pltpu.VMEM((4, 2, f_in, blk), BF16),
             pltpu.VMEM((2, 4) + piece, F32),
             pltpu.VMEM((4,) + piece, F32),
             pltpu.VMEM((4,) + piece, F32),
@@ -462,6 +488,7 @@
             pltpu.SemaphoreType.DMA((9,)),
             pltpu.SemaphoreType.DMA((LOTS,)),
             pltpu.SemaphoreType.DMA((ARRIVALS,)),
+            pltpu.SemaphoreType.DMA((4,)),
         ],
         compiler_params=pltpu.CompilerParams(
             collective_id=0, has_side_effects=True, vmem_limit_bytes=VMEM_BYTES

time: 72.1 us -> 71 us (0.985)
  Pallas kernels: 70.7 us -> 69.6 us
    pallas_call x1, Pallas kernels: 70 us -> 68.9 us  [per_device(): pl.pallas_call(layer_kernel, out_shape=(pltpu.VMEM((nodes, hid), BF16), p...]
where the time goes in v4:
time: 71 us; the launch traced here: 70.9 us
  Pallas kernels  69.6 us (98%)
  between operations  1.29 us (2%)
    pallas_call x1, Pallas kernels, per_device(): pl.pallas_call(layer_kernel, out_shape=(pltpu.VMEM((nodes, hid), BF16), p...  68.9 us

profile of v4, /device:TPU:1, one launch (start us, length us, event | category | flops | bytes accessed | tf_op | source)
XLA Modules:
  0.0 70.9 jit_solution(13036879901450462573)
XLA Ops:
  1.3 68.9 %graph_layer.1 = (bf16[256,256]{1,0:T(8,128)(2,1)S(1)}, bf16[256,128]{1,0:T(8,128)(2,1)S(1)}, f32[128,256]{1,0:T(8,128)S(1)}, f32[1,256]{1,0:T(1,128)S(1)}) custom-call(bf16[256,128]{1,0:T(8,128)(2,1)} %feat_hbm.1, bf16[128,256]{1,0:T(8,128)(2,1)} %weight_hbm.1, f32[1,256]{1,0:T(1,128)} %bitcast.6, bf16[256,256]{1,0:T(8,128)(2,1)} %cot_hbm.1, ...), custom_call_target="tpu_custom_call" | custom-call | tf_op jit(solution)/shard_map/graph_layer/pallas_call | solution.py:441
  70.2 0.8 %deliver.1 = (bf16[256,256]{1,0:T(8,128)(2,1)}, bf16[256,128]{1,0:T(8,128)(2,1)}, f32[128,256]{1,0:T(8,128)}, f32[1,256]{1,0:T(1,128)}) custom-call(bf16[256,256]{1,0:T(8,128)(2,1)S(1)} %get-tuple-element.12.refs_0_, bf16[256,128]{1,0:T(8,128)(2,1)S(1)} %get-tuple-element.13.refs_1_, f32[128,256]{1,0:T(8,128)S(1)} %get-tuple-element.14.refs_2_, ...), custom_call_target="tpu_custom_call" | custom-call | tf_op jit(solution)/shard_map/deliver/pallas_call | solution.py:507

commit v5 on v4

--- a/solution.py
+++ b/solution.py
@@ -186,14 +186,6 @@
     def ending(line, segment):
         return jnp.clip(table[line, segment], 0, slots)
 
-    def place(c, carry):
-        cx, cz, cy = c // 8, lax.rem(c // 4, 2), lax.rem(c, 4)
-        part[0, cy, cx, cz] = run[ending(3, c * 2)]
-        part[1, cx, cy, cz] = run[ending(3, c * 2 + 1)]
-        return carry
-
-    lax.fori_loop(0, 32, place, 0)
-
     big, small = (y, x), (x, y)
     at_big, at_small = (at_y, at_x), (at_x, at_y)
     layers = (1 - zh, zh)
@@ -203,6 +195,9 @@
     def issue(n, lay):
         for h in both:
             q = step4(small[h], OFFSETS[n])
+            for c in range(4):
+                device = (q * 8 + c if h == 0 else c * 8 + q) + layers[lay] * 4
+                part[h, c, q, layers[lay]] = run[ending(3, device * 2 + h)]
             for d in (2, 1, 3):
                 src = part.at[h, step4(big[h], d), q, layers[lay]]
                 send(src, landed.at[h, lay, n, d - 1], at_big[h](d), ("big", h, lay, n), 1 + lay)
@@ -363,15 +358,13 @@
     for d in (1, 2, 3):
         send(gw_y.at[y], gw_y.at[y], at_y(d), "gw y", 8)
     lax.fori_loop(middle, slots // UNROLL, backward, acc)
-    def place_back(r, carry):
+    def place_back(c, z):
         for b in range(2):
-            back[lax.rem(r, 2), r // 2, b] = run[ending(7, r * 2 + b)]
-        return carry
-
-    lax.fori_loop(0, 8, place_back, 0)
+            back[c, z, b] = run[ending(7, z * 4 + c * 2 + b)]
 
     near = []
     for n, other in enumerate((*chips, zl)):
+        place_back(1 - core, other)
         near.append(send(back.at[1 - core, other], back_in.at[n], sibling, ("back", n), 9))
     wait_all(gw_y.at[pl.ds(0, 3)], arrival("gw y"))
     piece = gw_y[0] + gw_y[1] + gw_y[2] + gw_y[3]
@@ -382,6 +375,8 @@
         send(mine, mine, at_row(other * 2 + core), "gw out", 10)
     send(mine, mine, sibling, "gw pass", 10)
 
+    for other in (*chips, zl):
+        place_back(core, other)
     for n, other in enumerate(chips):
         near[n].wait_recv()
         back_sum[n] = (back[core, other].astype(F32) + back_in[n].astype(F32)).astype(BF16)

time: 71 us -> 70 us (0.986)
  Pallas kernels: 69.6 us -> 68.7 us
    pallas_call x1, Pallas kernels: 68.9 us -> 67.9 us  [per_device(): pl.pallas_call(layer_kernel, out_shape=(pltpu.VMEM((nodes, hid), BF16), p...]
where the time goes in v5:
time: 70 us
  Pallas kernels  68.7 us (98%)
  between operations  1.29 us (2%)
    pallas_call x1, Pallas kernels, per_device(): pl.pallas_call(layer_kernel, out_shape=(pltpu.VMEM((nodes, hid), BF16), p...  67.9 us

profile of v5, /device:TPU:1, one launch (start us, length us, event | category | flops | bytes accessed | tf_op | source)
XLA Modules:
  0.0 70.0 jit_solution(15713154205169211330)
XLA Ops:
  1.3 67.9 %graph_layer.1 = (bf16[256,256]{1,0:T(8,128)(2,1)S(1)}, bf16[256,128]{1,0:T(8,128)(2,1)S(1)}, f32[128,256]{1,0:T(8,128)S(1)}, f32[1,256]{1,0:T(1,128)S(1)}) custom-call(bf16[256,128]{1,0:T(8,128)(2,1)} %feat_hbm.1, bf16[128,256]{1,0:T(8,128)(2,1)} %weight_hbm.1, f32[1,256]{1,0:T(1,128)} %bitcast.6, bf16[256,256]{1,0:T(8,128)(2,1)} %cot_hbm.1, ...), custom_call_target="tpu_custom_call" | custom-call | tf_op jit(solution)/shard_map/graph_layer/pallas_call | solution.py:436
  69.2 0.8 %deliver.1 = (bf16[256,256]{1,0:T(8,128)(2,1)}, bf16[256,128]{1,0:T(8,128)(2,1)}, f32[128,256]{1,0:T(8,128)}, f32[1,256]{1,0:T(1,128)}) custom-call(bf16[256,256]{1,0:T(8,128)(2,1)S(1)} %get-tuple-element.12.refs_0_, bf16[256,128]{1,0:T(8,128)(2,1)S(1)} %get-tuple-element.13.refs_1_, f32[128,256]{1,0:T(8,128)S(1)} %get-tuple-element.14.refs_2_, ...), custom_call_target="tpu_custom_call" | custom-call | tf_op jit(solution)/shard_map/deliver/pallas_call | solution.py:502

commit v6 on v5

--- a/solution.py
+++ b/solution.py
@@ -192,12 +192,16 @@
     both = (0, 1)
     copies = {}
 
-    def issue(n, lay):
+    def place(n, lay):
         for h in both:
             q = step4(small[h], OFFSETS[n])
             for c in range(4):
                 device = (q * 8 + c if h == 0 else c * 8 + q) + layers[lay] * 4
                 part[h, c, q, layers[lay]] = run[ending(3, device * 2 + h)]
+
+    def issue(n, lay):
+        for h in both:
+            q = step4(small[h], OFFSETS[n])
             for d in (2, 1, 3):
                 src = part.at[h, step4(big[h], d), q, layers[lay]]
                 send(src, landed.at[h, lay, n, d - 1], at_big[h](d), ("big", h, lay, n), 1 + lay)
@@ -229,7 +233,10 @@
                 halves[h] = total
 
     for n in range(4):
+        place(n, 0)
         issue(n, 0)
+    for n in range(4):
+        place(n, 1)
     for n in range(4):
         finish(n, 0)
         issue(n, 1)

time: 70 us -> 70.1 us (level)
  no operation moved by 1% of the time
where the time goes in v6:
time: 70.1 us; the launch traced here: 70 us
  Pallas kernels  68.7 us (98%)
  between operations  1.29 us (2%)
    pallas_call x1, Pallas kernels, per_device(): pl.pallas_call(layer_kernel, out_shape=(pltpu.VMEM((nodes, hid), BF16), p...  68 us

profile of v6, /device:TPU:1, one launch (start us, length us, event | category | flops | bytes accessed | tf_op | source)
XLA Modules:
  0.0 70.0 jit_solution(5900957438622829530)
XLA Ops:
  1.3 68.0 %graph_layer.1 = (bf16[256,256]{1,0:T(8,128)(2,1)S(1)}, bf16[256,128]{1,0:T(8,128)(2,1)S(1)}, f32[128,256]{1,0:T(8,128)S(1)}, f32[1,256]{1,0:T(1,128)S(1)}) custom-call(bf16[256,128]{1,0:T(8,128)(2,1)} %feat_hbm.1, bf16[128,256]{1,0:T(8,128)(2,1)} %weight_hbm.1, f32[1,256]{1,0:T(1,128)} %bitcast.6, bf16[256,256]{1,0:T(8,128)(2,1)} %cot_hbm.1, ...), custom_call_target="tpu_custom_call" | custom-call | tf_op jit(solution)/shard_map/graph_layer/pallas_call | solution.py:443
  69.2 0.8 %deliver.1 = (bf16[256,256]{1,0:T(8,128)(2,1)}, bf16[256,128]{1,0:T(8,128)(2,1)}, f32[128,256]{1,0:T(8,128)}, f32[1,256]{1,0:T(1,128)}) custom-call(bf16[256,256]{1,0:T(8,128)(2,1)S(1)} %get-tuple-element.12.refs_0_, bf16[256,128]{1,0:T(8,128)(2,1)S(1)} %get-tuple-element.13.refs_1_, f32[128,256]{1,0:T(8,128)S(1)} %get-tuple-element.14.refs_2_, ...), custom_call_target="tpu_custom_call" | custom-call | tf_op jit(solution)/shard_map/deliver/pallas_call | solution.py:509
